TPU v7x, 256 devices: a whole 4x4x8 slice. The times are simulated.
256 devices in a mesh: pole: 4 (over x), row: 8 (over y, z_hi), col: 8 (over z_lo, core).
Axes of the slice: x: 4, y: 4, z: 8 (z_hi: 2, z_lo: 4; z = z_hi * 4 + z_lo), core: 2. Of those that a mesh axis runs over, the one named last changes fastest.
Arguments:
- root_inverse: float32 [4, 2048, 2048], P('pole', 'row', 'col'), may hold values from -1 to 3
- top_factor: float32 [4, 2, 2048, 1024], P('pole', None, 'row', 'col'), may hold values from -0.125 to 0.125
- parent_factor: float32 [4, 4, 1024, 1024], P('pole', None, 'row', 'col'), may hold values from -0.109375 to 0.109375
- root_factor: float32 [4, 4, 2048, 1024], P('pole', None, 'row', 'col'), may hold values from -0.109375 to 0.109375
- top_pivots_inv: float32 [4, 2, 1024, 1024], P('pole', None, 'row', 'col'), may hold values from -1 to 3
- leaf_pivots_inv: float32 [4, 4, 1024, 1024], P('pole', None, 'row', 'col'), may hold values from -1 to 3
- pattern_top: int32 [2, 16], P(None, 'row'), may hold values 0 or 1
- pattern_parent: int32 [4, 8], P(None, 'row'), may hold values 0 or 1
- pattern_root: int32 [4, 16], P(None, 'row'), may hold values 0 or 1
- pole_weights: float32 [4], P('pole'), may hold values from 0.25 to 1
Outputs:
- density_top_diag: float32 [2, 1024, 1024], P(None, 'row', 'col')
- density_top_root: float32 [2, 2048, 1024], P(None, 'row', 'col')
- density_leaf_diag: float32 [4, 1024, 1024], P(None, 'row', 'col')
- density_leaf_parent: float32 [4, 1024, 1024], P(None, 'row', 'col')
- density_leaf_root: float32 [4, 2048, 1024], P(None, 'row', 'col')
All inputs are finite; a program needn't handle non-finite values. No bound on the sum of `pattern_top` or of `pattern_parent` or of `pattern_root` on one device may be relied on, other than what follows from the above.
Results may differ from a plain program's by a relative error of at most 0.00013.
Values sent between devices are 32-bit elements; how exact they have to be, the bound alone decides.
No kernel may reach another device: no remote copies, remote signals or barrier semaphores. Data moves between devices by JAX's collectives and lax.ppermute only.
A program may use at most 64 MiB of HBM per device.

v0:
```python
import math

import jax
import jax.numpy as jnp
from jax import lax
from jax.experimental import pallas as pl
from jax.experimental.pallas import tpu as pltpu
from jax.sharding import Mesh
from jax.sharding import PartitionSpec as P

RING = ("zh", "zl")
LANE = ("zh", "zl", "core")
PLANE = ("y", "zh", "zl", "core")
SIZE_X, SIZE_Y, SIZE_H, SIZE_L, SIZE_C = 4, 4, 2, 4, 2
SIZE_Z = SIZE_H * SIZE_L
VMEM = pltpu.CompilerParams(vmem_limit_bytes=64 * 1024 * 1024)
IN_VMEM = pl.BlockSpec(memory_space=pltpu.VMEM)
IN_SMEM = pl.BlockSpec(memory_space=pltpu.SMEM)


def block_mask(pattern, rows):
    width = rows // pattern.shape[-1]
    return jnp.repeat(pattern.astype(jnp.float32), width, axis=-1)


def lane_pairs(target):
    pairs = []
    for zh in range(SIZE_H):
        for zl in range(SIZE_L):
            for core in range(SIZE_C):
                to_h, to_l, to_c = target(zh, zl, core)
                pairs.append(
                    ((zh * SIZE_L + zl) * SIZE_C + core, (to_h * SIZE_L + to_l) * SIZE_C + to_c)
                )
    return pairs


def plane_pairs(flip):
    pairs = []
    for y in range(SIZE_Y):
        for zh in range(SIZE_H):
            for zl in range(SIZE_L):
                for core in range(SIZE_C):
                    here = ((y * SIZE_H + zh) * SIZE_L + zl) * SIZE_C + core
                    there = ((zl * SIZE_H + zh) * SIZE_L + y) * SIZE_C + (core ^ flip)
                    pairs.append((here, there))
    return pairs


def ring_pairs(step):
    return [(z, (z + step) % SIZE_Z) for z in range(SIZE_Z)]


def onward(pieces, step):
    ahead, behind = (pieces[-2], pieces[-1]) if step else (pieces[0], pieces[0])
    if step == 3:
        half = ahead.shape[0] // 2
        ahead, behind = ahead[:half], behind[half:]
    return [
        lax.ppermute(ahead, RING, ring_pairs(1)),
        lax.ppermute(behind, RING, ring_pairs(-1)),
    ]


def column_of(place):
    return (place % SIZE_L) * SIZE_H + place // SIZE_L


def spread(value, axis, size):
    return lax.all_to_all(jnp.broadcast_to(value[None], (size,) + value.shape), axis, 0, 0)


def in_order(flag, first, second):
    return jnp.where(flag == 0, first, second), jnp.where(flag == 0, second, first)


def split(value):
    high = value.astype(jnp.bfloat16)
    return high, (value - high.astype(jnp.float32)).astype(jnp.bfloat16)


def product(left, right, dims=((1,), (0,))):
    def one(a, b):
        return lax.dot_general(a, b, (dims, ((), ())), preferred_element_type=jnp.float32)

    return one(left[0], right[0]) + (one(left[0], right[1]) + one(left[1], right[0]))


def product_t(left, right):
    return product(left, right, ((0,), (0,)))


def fetched(sources, scratch, sems):
    copies = [
        pltpu.make_async_copy(source, to, sems.at[at])
        for at, (source, to) in enumerate(zip(sources, scratch))
    ]
    for copy in copies:
        copy.start()

    def ready(at):
        copies[at].wait()
        return scratch[at]

    return ready


def outer_kernel(inverse, top, out, inverse_here, top_here, sems):
    order = [half * 8 + k for k in range(8) for half in range(2)]
    ready = fetched(
        [top.at[:, 0:256, :]] + [inverse.at[at] for at in order],
        [top_here.at[:, 0:256, :]] + [inverse_here.at[at] for at in order],
        sems,
    )
    ready(0)
    totals = [None, None]
    for k in range(8):
        right = split(top_here[k, 0:256, :])
        for half in range(2):
            left = split(ready(1 + k * 2 + half)[...])
            part = product(left, right)
            totals[half] = part if k == 0 else totals[half] + part
    for half in range(2):
        out[half * 256 : (half + 1) * 256, :] = -totals[half]


def cross_kernel(order, *refs):
    sources, (top_out, leaf_out) = refs[:10], refs[10:12]
    scratch, sems = refs[12:22], refs[22]
    ready = fetched(sources, scratch, sems)
    mine = ready(0)
    panels = split(
        jnp.concatenate(
            [
                jnp.concatenate(
                    [mine[zh, 0:256, :], mine[zh, 512:768, :], mine[zh, 768:1024, :]], axis=1
                )
                for zh in range(SIZE_H)
            ],
            axis=0,
        )
    )
    for at in range(8):
        if at < 7:
            piece = ready(1 + at)[...]
        else:
            piece = jnp.concatenate([ready(8)[...], ready(9)[...]], axis=0)
        part = product_t(split(piece), panels)
        top_out[order[at]] = part[:, :128]
        leaf_out[order[at], 0] = part[:, 128:256]
        leaf_out[order[at], 1] = part[:, 256:]


def root_kernel(order, *refs):
    sources, out = refs[:12], refs[12]
    scratch, sems = refs[13:25], refs[25]
    ready = fetched(sources, scratch, sems)
    cols, last, inverse = ready(0), ready(1), ready(2)
    totals = [jnp.zeros((256, 256), jnp.float32) for _ in range(2)]
    for k in range(8):
        root = split(jnp.concatenate([cols[k, 512:768, :], last[k]], axis=1))
        for half in range(2):
            totals[half] += product(split(inverse[half * 8 + k]), root)
    for at in range(8):
        if at < 7:
            piece = ready(3 + at)[...]
        else:
            piece = jnp.concatenate([ready(10)[...], ready(11)[...]], axis=0)
        place = order[at]
        parent = split(
            jnp.concatenate([cols[place, 256:384, :], cols[place, 384:512, :]], axis=1)
        )
        for half in range(2):
            totals[half] += product(split(piece[half * 256 : (half + 1) * 256]), parent)
    for half in range(2):
        for leaf in range(2):
            out[leaf, half * 256 : (half + 1) * 256, :] = -totals[half][
                :, leaf * 128 : (leaf + 1) * 128
            ]


def parent_kernel(order, *refs):
    sources, out, scratch, sems = refs[:11], refs[11], refs[12:23], refs[23]
    ready = fetched(sources, scratch, sems)
    cols, cross = ready(0), ready(1)
    total = jnp.zeros((256, 256), jnp.float32)
    for at in range(8):
        if at < 7:
            piece = ready(2 + at)[...]
        else:
            piece = jnp.concatenate([ready(9)[...], ready(10)[...]], axis=0)
        place = order[at]
        parent = jnp.concatenate([cols[place, 256:384, :], cols[place, 384:512, :]], axis=1)
        total += product(split(piece), split(parent))
    for leaf in range(2):
        for sub in range(2):
            added = cross[0, sub, leaf]
            for y in range(1, SIZE_Y):
                added += cross[y, sub, leaf]
            rows = slice(sub * 128, (sub + 1) * 128)
            out[leaf, rows, :] = -(total[rows, leaf * 128 : (leaf + 1) * 128] + added)


def leaf_kernel(core, weight, parent, root, panels, out, total, high, low):
    block, half = pl.program_id(0), pl.program_id(1)

    @pl.when(block == 0)
    def _():
        for leaf in range(2):
            rows = jnp.concatenate([parent[leaf], root[leaf]], axis=0)
            high[half, leaf], low[half, leaf] = split(jnp.transpose(rows))

    for leaf in range(2):
        right = split(jnp.concatenate([panels[0, leaf], panels[1, leaf]], axis=1))
        part = product((high[half, leaf], low[half, leaf]), right)

        @pl.when(half == 0)
        def _():
            total[leaf] = part

        @pl.when(half == 1)
        def _():
            done = weight[0] * (total[leaf] + part)
            for side in range(2):
                out[:, 0, side, leaf] = done[:, side * 128 : (side + 1) * 128].reshape(
                    SIZE_X, 32, 128
                )


def leaf_cross(core, weight, parent, root, panels):
    return pl.pallas_call(
        leaf_kernel,
        out_shape=jax.ShapeDtypeStruct((SIZE_X, SIZE_Y, 2, 2, 32, 128), jnp.float32),
        grid_spec=pltpu.PrefetchScalarGridSpec(
            num_scalar_prefetch=1,
            grid=(SIZE_L, SIZE_H),
            in_specs=[
                IN_SMEM,
                pl.BlockSpec((2, 128, 128), lambda l, h, core: (0, h, 0)),
                pl.BlockSpec((2, 256, 128), lambda l, h, core: (0, h, 0)),
                pl.BlockSpec((2, 2, 384, 128), lambda l, h, core: (h * 4 + l, core[0], 0, 0)),
            ],
            out_specs=pl.BlockSpec(
                (SIZE_X, 1, 2, 2, 32, 128), lambda l, h, core: (0, l, 0, 0, 0, 0)
            ),
            scratch_shapes=[
                pltpu.VMEM((2, 128, 256), jnp.float32),
                pltpu.VMEM((2, 2, 128, 384), jnp.bfloat16),
                pltpu.VMEM((2, 2, 128, 384), jnp.bfloat16),
            ],
        ),
        cost_estimate=cost(2 * 768 * 1024 * 128, [(2, 768, 1024), (2, 768, 128), (2, 1024, 128)]),
        compiler_params=VMEM,
    )(core, weight, parent, root, panels)


def cost(terms, arrays):
    moved = 4 * sum(math.prod(shape) for shape in arrays)
    return pl.CostEstimate(flops=6 * terms, bytes_accessed=moved, transcendentals=0)


def with_copies(kernel, shapes, order, *operands, terms, copies=None):
    specs = [pl.BlockSpec(memory_space=pl.ANY)] * len(operands)
    scratch = [pltpu.VMEM(operand.shape, jnp.float32) for operand in operands]
    scratch.append(pltpu.SemaphoreType.DMA((copies or len(operands),)))
    price = cost(terms, [operand.shape for operand in operands] + shapes)
    if order is not None:
        specs, operands = [IN_SMEM] + specs, (order,) + operands
    return pl.pallas_call(
        kernel,
        out_shape=[jax.ShapeDtypeStruct(shape, jnp.float32) for shape in shapes],
        in_specs=specs,
        out_specs=[IN_VMEM] * len(shapes),
        scratch_shapes=scratch,
        cost_estimate=price,
        compiler_params=VMEM,
    )(*operands)


def body(
    root_inverse,
    top_factor,
    parent_factor,
    root_factor,
    top_pivots_inv,
    leaf_pivots_inv,
    pattern_top,
    pattern_parent,
    pattern_root,
    pole_weights,
):
    zh = lax.axis_index("zh")
    zl = lax.axis_index("zl")
    core = lax.axis_index("core")
    place = zh * SIZE_L + zl
    weight = pole_weights[0]

    top = top_factor[0] * block_mask(pattern_top, 256)[:, :, None]
    parent = parent_factor[0] * block_mask(pattern_parent, 128)[:, :, None]
    root = root_factor[0] * block_mask(pattern_root, 256)[:, :, None]

    leaves = jnp.concatenate([parent, root], axis=1)

    def to_ring(value):
        got = []
        for flip in range(2):
            piece = lax.dynamic_index_in_dim(value, zh ^ flip, 0, keepdims=False)
            got.append(
                lax.ppermute(piece, LANE, lane_pairs(lambda h, l, c: (c, l, h ^ flip)))
            )
        return jnp.stack(in_order(core, got[0], got[1]))

    block = to_ring(
        jnp.concatenate(
            [top, parent.reshape(2, 256, 128), root.reshape(2, 512, 128), top_pivots_inv[0]],
            axis=1,
        )
    )
    pivot_block = block[:, 1024:].reshape(256, 128)
    first_cols = spread(block[:, :768], "y", SIZE_Y).reshape(8, 768, 128)
    inverse, block = lax.optimization_barrier((root_inverse[0], block))
    inverse = lax.all_gather(inverse, LANE, axis=0)

    leaf = (weight * leaf_pivots_inv[0]).reshape(4, SIZE_X, 32, 128)
    leaf = jnp.sum(lax.all_to_all(jnp.moveaxis(leaf, 1, 0), "pole", 0, 0), axis=0)
    first_cols, leaf = lax.optimization_barrier((first_cols, leaf))

    (outer,) = with_copies(
        outer_kernel,
        [(512, 128)],
        None,
        inverse,
        first_cols,
        terms=512 * 2048 * 128,
        copies=17,
    )
    last_cols = spread(block[:, 768:1024], "y", SIZE_Y).reshape(8, 256, 128)
    pieces = [outer]
    for step in range(3):
        pieces += onward(pieces, step)
    pieces[5], pieces[6], leaves, last_cols = lax.optimization_barrier(
        (pieces[5], pieces[6], leaves, last_cols)
    )
    pieces += onward(pieces, 3)
    panels = lax.all_gather(leaves, LANE, axis=0)
    order = jnp.stack([column_of((place + d) % SIZE_Z) for d in (0, 7, 1, 6, 2, 5, 3, 4)])

    cross_top, cross_leaf = with_copies(
        cross_kernel,
        [(8, 128, 128), (8, 2, 128, 128)],
        order,
        block,
        *pieces,
        terms=512 * 1024 * 384,
    )
    cross_leaf, last_cols = lax.optimization_barrier((cross_leaf, last_cols))
    (leaf_root,) = with_copies(
        root_kernel,
        [(2, 512, 128)],
        order,
        first_cols,
        last_cols,
        inverse,
        *pieces,
        terms=512 * 3072 * 256,
    )
    cross_top = lax.all_to_all(cross_top.reshape(SIZE_Y, 256, 128), "y", 0, 0)
    cross_top, cross_leaf, leaf_root = lax.optimization_barrier(
        (cross_top, cross_leaf, leaf_root)
    )
    cross_leaf = lax.all_to_all(cross_leaf.reshape(SIZE_Y, 2, 2, 128, 128), "y", 0, 0)
    top_diag = pivot_block - jnp.sum(cross_top, axis=0)
    def summed(values):
        blocks = jnp.concatenate(
            [value.reshape(SIZE_H, value.shape[0] // SIZE_H, 128) for value in values], axis=1
        )
        blocks = (weight * blocks).reshape(SIZE_H, SIZE_X, blocks.shape[1] // SIZE_X, 128)
        return jnp.sum(lax.all_to_all(jnp.moveaxis(blocks, 1, 0), "pole", 0, 0), axis=0)

    def in_place(blocks):
        got = []
        for flip in range(2):
            piece = lax.dynamic_index_in_dim(blocks, core ^ flip, 0, keepdims=False)
            got.append(
                lax.ppermute(piece, LANE, lane_pairs(lambda h, l, c: (c ^ flip, l, h)))
            )
        return jnp.stack(in_order(zh, got[0], got[1]), axis=0)

    def everywhere(pair):
        every = jnp.moveaxis(spread(pair, "pole", SIZE_X), 0, 1)
        return every.reshape(pair.shape[0], SIZE_X * pair.shape[1], 128)

    diag_pieces = [top_diag]
    for step in range(3):
        diag_pieces += onward(diag_pieces, step)
    early = summed([outer, leaf_root[0], leaf_root[1]])
    diag_pieces[5], diag_pieces[6], early = lax.optimization_barrier(
        (diag_pieces[5], diag_pieces[6], early)
    )
    diag_pieces += onward(diag_pieces, 3)
    early = in_place(early)
    diag_pieces[7], diag_pieces[8], early = lax.optimization_barrier(
        (diag_pieces[7], diag_pieces[8], early)
    )
    (leaf_parent,) = with_copies(
        parent_kernel,
        [(2, 256, 128)],
        order,
        first_cols,
        cross_leaf,
        *diag_pieces,
        terms=256 * 1024 * 256,
    )
    early = everywhere(early)
    late = summed([top_diag, leaf_parent[0], leaf_parent[1]])

    cross = leaf_cross(core.reshape(1), pole_weights, leaf_parent, leaf_root, panels)
    cross, early = lax.optimization_barrier((cross, early))
    cross = cross.reshape(SIZE_X * SIZE_Y, 2, 2, 32, 128)
    cross = jnp.sum(lax.all_to_all(cross, ("pole", "y"), 0, 0), axis=0)
    late = in_place(late)
    got = []
    for flip in range(2):
        piece = lax.dynamic_index_in_dim(cross, core ^ flip, 0, keepdims=False)
        got.append(lax.ppermute(piece, PLANE, plane_pairs(flip)))
    cross = jnp.concatenate(in_order(core, got[0], got[1]), axis=0)
    ends = everywhere(jnp.concatenate([late.reshape(6, 32, 128), leaf - cross], axis=0))
    outer_dens = early[:, :256]
    rootward_dens = early[:, 256:].reshape(4, 256, 128)
    leaf_dens = ends[6:]
    late = jnp.moveaxis(ends[:6].reshape(2, 3, SIZE_X, 32, 128), 2, 1).reshape(2, 384, 128)
    top_dens = late[:, :128]
    parent_dens = late[:, 128:].reshape(4, 128, 128)
    return (top_dens, outer_dens, leaf_dens, parent_dens, rootward_dens)


def solution(mesh):
    fine = Mesh(
        mesh.devices.reshape(SIZE_X, SIZE_Y, SIZE_H, SIZE_L, SIZE_C),
        ("pole", "y", "zh", "zl", "core"),
    )
    row, col = ("y", "zh"), ("zl", "core")
    return jax.shard_map(
        body,
        mesh=fine,
        in_specs=(
            P("pole", row, col),
            P("pole", None, row, col),
            P("pole", None, row, col),
            P("pole", None, row, col),
            P("pole", None, row, col),
            P("pole", None, row, col),
            P(None, row),
            P(None, row),
            P(None, row),
            P("pole"),
        ),
        out_specs=(
            P(None, row, col),
            P(None, row, col),
            P(None, row, col),
            P(None, row, col),
            P(None, row, col),
        ),
        check_vma=False,
    )
```

profile of v0, /device:TPU:24, one launch (start us, length us, event | category | flops | bytes accessed | tf_op | source)
XLA Modules:
  0.0 303.6 jit_solution(1380403499555583894)
XLA Ops:
  12.3 15.7 %collective-permute-done.1 = f32[1152,128]{1,0:T(8,128)S(1)} collective-permute-done((f32[1152,128]{1,0:T(8,128)S(1)}, f32[1152,128]{1,0:T(8,128)S(1)}, u32[]{:S(2)}, u32[]{:S(2)}) %collective-permute-start.1) | collective-permute-done | bytes 589856 | tf_op jit(solution)/shard_map/ppermute | solution.py:309
  35.0 6.6 %all-to-all-done.1 = f32[4,4,32,128]{3,2,1,0:T(8,128)S(1)} async-done(((f32[4,4,32,128]{3,2,1,0:T(8,128)}), f32[4,4,32,128]{3,2,1,0:T(8,128)S(1)}, u32[]{:S(2)}, u32[]{:S(2)}) %all-to-all-start.1) | async-done | bytes 262176 | tf_op jit(solution)/shard_map/all_to_all | solution.py:325
  43.4 6.8 %all-to-all-start = ((f32[4,2,768,128]{3,2,1,0:T(8,128)}), f32[4,2,768,128]{3,2,1,0:T(8,128)}, u32[]{:S(2)}, u32[]{:S(2)}) async-start(f32[4,2,768,128]{3,2,1,0:T(8,128)} %broadcast_in_dim.14), calls=%async_computation | async-start | bytes 6291456 | tf_op jit(solution)/shard_map/all_to_all | solution.py:70
  50.9 28.7 %all-to-all-done = f32[4,2,768,128]{3,2,1,0:T(8,128)} async-done(((f32[4,2,768,128]{3,2,1,0:T(8,128)}), f32[4,2,768,128]{3,2,1,0:T(8,128)}, u32[]{:S(2)}, u32[]{:S(2)}) %all-to-all-start) | async-done | bytes 3145760 | tf_op jit(solution)/shard_map/all_to_all | solution.py:70
  79.6 8.9 %all-gather.5.cloned.1.call-done = f32[4096,256]{1,0:T(8,128)} async-done(((f32[256,256]{1,0:T(8,128)}), f32[4096,256]{1,0:T(8,128)}) %all-gather.5.cloned.1.call-update) | async-done | bytes 4194320 | tf_op jit(solution)/shard_map/all_gather | solution.py:322
  88.5 6.8 %shard_map.137.refs_1_.refs_3_ = f32[512,128]{1,0:T(8,128)} custom-call(f32[16,256,256]{2,1,0:T(8,128)} %bitcast.107, f32[8,768,128]{2,1,0:T(8,128)} %bitcast.19.top.refs_0_), custom_call_target="tpu_custom_call" | custom-call | flops 805306368 | bytes 7602176 | tf_op jit(solution)/shard_map/pallas_call | solution.py:269
  96.6 7.1 %collective-permute-start.3 = (f32[512,128]{1,0:T(8,128)}, f32[512,128]{1,0:T(8,128)S(1)}, u32[]{:S(2)}, u32[]{:S(2)}) collective-permute-start(f32[512,128]{1,0:T(8,128)} %shard_map.137.refs_1_.refs_3_), channel_id=1, source_target_pairs={{0,14},{2,0},{4,2},{6,4},{8,6},{10,8},{12,10},{14,12},{1,15},{3,1}... | collective-permute-start | bytes 786440 | tf_op jit(solution)/shard_map/ppermute | solution.py:61
  106.5 6.4 %all-to-all-start.2 = ((f32[4,2,256,128]{3,2,1,0:T(8,128)}), f32[4,2,256,128]{3,2,1,0:T(8,128)}, u32[]{:S(2)}, u32[]{:S(2)}) async-start(f32[4,2,256,128]{3,2,1,0:T(8,128)} %broadcast_in_dim.15), calls=%async_computation.2 | async-start | bytes 2097152 | tf_op jit(solution)/shard_map/all_to_all | solution.py:70
  136.9 6.6 %shard_map.138 = (f32[8,128,128]{2,1,0:T(8,128)}, f32[8,2,128,128]{3,2,1,0:T(8,128)}) custom-call(s32[8]{0:T(128)} %stack.65.order, f32[2,1152,128]{2,1,0:T(8,128)} %pad_maximum_fusion.refs_0_, f32[512,128]{1,0:T(8,128)} %shard_map.137.refs_1_.refs_3_, f32[512,128]{1,0:T(8,128)} %copy-done.15, f32[512,128]{1,0:T(8,128)} %copy-done.16, ...), custom_call_target="tpu_custom_call" | custom-call | flops 1207959552 | bytes 4849664 | tf_op jit(solution)/shard_map/pallas_call | solution.py:269
  143.5 4.9 %all-to-all-start.3 = ((f32[4,256,128]{2,1,0:T(8,128)}), f32[4,256,128]{2,1,0:T(8,128)}, u32[]{:S(2)}, u32[]{:S(2)}) async-start(f32[4,256,128]{2,1,0:T(8,128)} %bitcast.128), calls=%async_computation.3 | async-start | bytes 1048576 | tf_op jit(solution)/shard_map/all_to_all | solution.py:367
  148.4 8.9 %shard_map.139.root = f32[2,512,128]{2,1,0:T(8,128)} custom-call(s32[8]{0:T(128)} %stack.65.order, f32[8,768,128]{2,1,0:T(8,128)} %bitcast.19.top.refs_0_, f32[8,256,128]{2,1,0:T(8,128)} %bitcast.25.refs_1_, f32[16,256,256]{2,1,0:T(8,128)} %bitcast.108, f32[512,128]{1,0:T(8,128)} %shard_map.137.refs_1_.refs_3_, f32[512,128]{1,0:T(8,128)} %copy-done.15, ...), custom_call_target="tpu_custom_call" | custom-call | flops 2415919104 | bytes 11010048 | tf_op jit(solution)/shard_map/pallas_call | solution.py:269
  168.3 6.3 %collective-permute-done.10.refs_3_ = f32[256,128]{1,0:T(8,128)S(1)} collective-permute-done((f32[256,128]{1,0:T(8,128)S(1)}, f32[256,128]{1,0:T(8,128)S(1)}, u32[]{:S(2)}, u32[]{:S(2)}) %collective-permute-start.10) | collective-permute-done | bytes 131104 | tf_op jit(solution)/shard_map/ppermute | solution.py:60
  177.9 4.8 %all-to-all-start.4 = ((f32[4,2,2,128,128]{4,3,2,1,0:T(8,128)}), f32[4,2,2,128,128]{4,3,2,1,0:T(8,128)S(1)}, u32[]{:S(2)}, u32[]{:S(2)}) async-start(f32[4,2,2,128,128]{4,3,2,1,0:T(8,128)} %bitcast.28), calls=%async_computation.4 | async-start | bytes 2097152 | tf_op jit(solution)/shard_map/all_to_all | solution.py:371
  187.4 5.8 %collective-permute-done.14.refs_7_ = f32[256,128]{1,0:T(8,128)S(1)} collective-permute-done((f32[256,128]{1,0:T(8,128)S(1)}, f32[256,128]{1,0:T(8,128)S(1)}, u32[]{:S(2)}, u32[]{:S(2)}) %collective-permute-start.14) | collective-permute-done | bytes 131104 | tf_op jit(solution)/shard_map/ppermute | solution.py:60
  193.8 5.7 %collective-permute-start.19 = (f32[192,128]{1,0:T(8,128)S(1)}, f32[192,128]{1,0:T(8,128)S(1)}, u32[]{:S(2)}, u32[]{:S(2)}) collective-permute-start(f32[192,128]{1,0:T(8,128)S(1)} %get-tuple-element.64), channel_id=1, source_target_pairs={{0,8},{1,0},{2,10},{3,2},{4,12},{5,4},{6,14},{7,6},{8,9},{9,1},{10... | collective-permute-start | bytes 294920 | tf_op jit(solution)/shard_map/ppermute | solution.py:385
  210.0 4.5 %all-to-all-start.7 = ((f32[4,2,192,128]{3,2,1,0:T(8,128)}), f32[4,2,192,128]{3,2,1,0:T(8,128)}, u32[]{:S(2)}, u32[]{:S(2)}) async-start(f32[4,2,192,128]{3,2,1,0:T(8,128)} %broadcast_in_dim.16), calls=%async_computation.7 | async-start | bytes 1572864 | tf_op jit(solution)/shard_map/all_to_all | solution.py:70
  214.5 5.7 %shard_map.140.parent = f32[2,256,128]{2,1,0:T(8,128)} custom-call(s32[8]{0:T(128)} %stack.65.order, f32[8,768,128]{2,1,0:T(8,128)} %bitcast.19.top.refs_0_, f32[4,2,2,128,128]{4,3,2,1,0:T(8,128)} %copy-done.4, f32[256,128]{1,0:T(8,128)} %copy-done.12, f32[256,128]{1,0:T(8,128)} %copy-done.23, f32[256,128]{1,0:T(8,128)} %copy-done.24, ...), custom_call_target="tpu_custom_call" | custom-call | flops 402653184 | bytes 5505024 | tf_op jit(solution)/shard_map/pallas_call | solution.py:269
  222.9 5.1 %all-to-all-done.7 = f32[4,2,192,128]{3,2,1,0:T(8,128)} async-done(((f32[4,2,192,128]{3,2,1,0:T(8,128)}), f32[4,2,192,128]{3,2,1,0:T(8,128)}, u32[]{:S(2)}, u32[]{:S(2)}) %all-to-all-start.7) | async-done | bytes 786464 | tf_op jit(solution)/shard_map/all_to_all | solution.py:70
  234.3 10.3 %shard_map.141 = f32[4,4,2,2,32,128]{5,4,3,2,1,0:T(8,128)} custom-call(s32[1]{0:T(128)} %bitcast.48.core, f32[1]{0:T(128)} %copy.40.weight, f32[2,256,128]{2,1,0:T(8,128)} %shard_map.140.parent, f32[2,512,128]{2,1,0:T(8,128)} %shard_map.139.root, f32[16,4,384,128]{3,2,1,0:T(8,128)} %bitcast.109), custom_call_target="tpu_custom_call" | custom-call | flops 1207959552 | bytes 8126464 | tf_op jit(solution)/shard_map/pallas_call | solution.py:231
  244.5 7.7 %all-to-all-start.8 = ((f32[16,2,2,32,128]{4,3,2,1,0:T(8,128)}), f32[16,2,2,32,128]{4,3,2,1,0:T(8,128)S(1)}, u32[]{:S(2)}, u32[]{:S(2)}) async-start(f32[16,2,2,32,128]{4,3,2,1,0:T(8,128)} %bitcast.110), calls=%async_computation.8 | async-start | bytes 2097152 | tf_op jit(solution)/shard_map/all_to_all | solution.py:420
  254.0 6.1 %collective-permute-start.21 = (f32[96,128]{1,0:T(8,128)S(1)}, f32[96,128]{1,0:T(8,128)S(1)}, u32[]{:S(2)}, u32[]{:S(2)}) collective-permute-start(f32[96,128]{1,0:T(8,128)S(1)} %get-tuple-element.68), channel_id=1, source_target_pairs={{0,8},{1,0},{2,10},{3,2},{4,12},{5,4},{6,14},{7,6},{8,9},{9,1},{10... | collective-permute-start | bytes 147464 | tf_op jit(solution)/shard_map/ppermute | solution.py:385
  261.9 5.0 %all-to-all-done.8 = f32[16,2,2,32,128]{4,3,2,1,0:T(8,128)S(1)} async-done(((f32[16,2,2,32,128]{4,3,2,1,0:T(8,128)}), f32[16,2,2,32,128]{4,3,2,1,0:T(8,128)S(1)}, u32[]{:S(2)}, u32[]{:S(2)}) %all-to-all-start.8) | async-done | bytes 1048608 | tf_op jit(solution)/shard_map/all_to_all | solution.py:420
  267.1 6.8 %collective-permute-start.22 = (f32[2,32,128]{2,1,0:T(8,128)S(1)}, f32[2,32,128]{2,1,0:T(8,128)S(1)}, u32[]{:S(2)}, u32[]{:S(2)}) collective-permute-start(f32[2,32,128]{2,1,0:T(8,128)S(1)} %get-tuple-element.71), channel_id=1, source_target_pairs={{0,0},{1,1},{2,16},{3,17},{4,32},{5,33},{6,48},{7,49},{8,8},{9,9},... | collective-permute-start | bytes 98312 | tf_op jit(solution)/shard_map/ppermute | solution.py:425
  287.3 7.2 %all-to-all-done.9 = f32[4,10,32,128]{3,2,1,0:T(8,128)S(1)} async-done(((f32[4,10,32,128]{3,2,1,0:T(8,128)}), f32[4,10,32,128]{3,2,1,0:T(8,128)S(1)}, u32[]{:S(2)}, u32[]{:S(2)}) %all-to-all-start.9) | async-done | bytes 655392 | tf_op jit(solution)/shard_map/all_to_all | solution.py:70
  (185 shorter events, 99.7 us)
Async XLA Ops:
  7.2 81.3 %all-gather.5.cloned.1.call-start = ((), (), s32[]{:S(2)}) async-start(), calls=%async_computation.10 | async-start | bytes 4456448 | tf_op jit(solution)/shard_map/all_gather | solution.py:322
  11.4 16.5 %collective-permute-start.1 = (f32[1152,128]{1,0:T(8,128)S(1)}, f32[1152,128]{1,0:T(8,128)S(1)}, u32[]{:S(2)}, u32[]{:S(2)}) collective-permute-start(f32[1152,128]{1,0:T(8,128)S(1)} %get-tuple-element.55), channel_id=1, source_target_pairs={{0,1},{1,9},{2,3},{3,11},{4,5},{5,13},{6,7},{7,15},{8,0},{9,8},{10... | collective-permute-start | bytes 1769480 | tf_op jit(solution)/shard_map/ppermute | solution.py:309
  11.5 16.4 %collective-permute-start = (f32[1152,128]{1,0:T(8,128)S(1)}, f32[1152,128]{1,0:T(8,128)S(1)}, u32[]{:S(2)}, u32[]{:S(2)}) collective-permute-start(f32[1152,128]{1,0:T(8,128)S(1)} %get-tuple-element.56), channel_id=1, source_target_pairs={{0,0},{1,8},{2,2},{3,10},{4,4},{5,12},{6,6},{7,14},{8,1},{9,9},{10... | collective-permute-start | bytes 1769480 | tf_op jit(solution)/shard_map/ppermute | solution.py:309
  30.6 11.0 %all-to-all-start.1 = ((f32[4,4,32,128]{3,2,1,0:T(8,128)}), f32[4,4,32,128]{3,2,1,0:T(8,128)S(1)}, u32[]{:S(2)}, u32[]{:S(2)}) async-start(f32[4,4,32,128]{3,2,1,0:T(8,128)} %copy.21), calls=%async_computation.1 | async-start | bytes 524288 | tf_op jit(solution)/shard_map/all_to_all | solution.py:325
  43.4 36.1 %all-to-all-start = ((f32[4,2,768,128]{3,2,1,0:T(8,128)}), f32[4,2,768,128]{3,2,1,0:T(8,128)}, u32[]{:S(2)}, u32[]{:S(2)}) async-start(f32[4,2,768,128]{3,2,1,0:T(8,128)} %broadcast_in_dim.14), calls=%async_computation | async-start | bytes 6291456 | tf_op jit(solution)/shard_map/all_to_all | solution.py:70
  95.3 17.6 %collective-permute-start.2 = (f32[512,128]{1,0:T(8,128)}, f32[512,128]{1,0:T(8,128)S(1)}, u32[]{:S(2)}, u32[]{:S(2)}) collective-permute-start(f32[512,128]{1,0:T(8,128)} %shard_map.137.refs_1_.refs_3_), channel_id=1, source_target_pairs={{0,2},{2,4},{4,6},{6,8},{8,10},{10,12},{12,14},{14,0},{1,3},{3,5},... | collective-permute-start | bytes 786440 | tf_op jit(solution)/shard_map/ppermute | solution.py:60
  96.6 16.4 %collective-permute-start.3 = (f32[512,128]{1,0:T(8,128)}, f32[512,128]{1,0:T(8,128)S(1)}, u32[]{:S(2)}, u32[]{:S(2)}) collective-permute-start(f32[512,128]{1,0:T(8,128)} %shard_map.137.refs_1_.refs_3_), channel_id=1, source_target_pairs={{0,14},{2,0},{4,2},{6,4},{8,6},{10,8},{12,10},{14,12},{1,15},{3,1}... | collective-permute-start | bytes 786440 | tf_op jit(solution)/shard_map/ppermute | solution.py:61
  106.5 18.6 %all-to-all-start.2 = ((f32[4,2,256,128]{3,2,1,0:T(8,128)}), f32[4,2,256,128]{3,2,1,0:T(8,128)}, u32[]{:S(2)}, u32[]{:S(2)}) async-start(f32[4,2,256,128]{3,2,1,0:T(8,128)} %broadcast_in_dim.15), calls=%async_computation.2 | async-start | bytes 2097152 | tf_op jit(solution)/shard_map/all_to_all | solution.py:70
  112.8 121.4 %all-gather.7.cloned.1.call-start = ((), (), s32[]{:S(2)}) async-start(), calls=%async_computation.11 | async-start | bytes 13369344 | tf_op jit(solution)/shard_map/all_gather | solution.py:345
  143.5 13.9 %all-to-all-start.3 = ((f32[4,256,128]{2,1,0:T(8,128)}), f32[4,256,128]{2,1,0:T(8,128)}, u32[]{:S(2)}, u32[]{:S(2)}) async-start(f32[4,256,128]{2,1,0:T(8,128)} %bitcast.128), calls=%async_computation.3 | async-start | bytes 1048576 | tf_op jit(solution)/shard_map/all_to_all | solution.py:367
  160.6 17.3 %all-to-all-start.5 = ((f32[4,2,192,128]{3,2,1,0:T(8,128)}), f32[4,2,192,128]{3,2,1,0:T(8,128)S(1)}, u32[]{:S(2)}, u32[]{:S(2)}) async-start(f32[4,2,192,128]{3,2,1,0:T(8,128)} %copy.22), calls=%async_computation.5 | async-start | bytes 1572864 | tf_op jit(solution)/shard_map/all_to_all | solution.py:378
  164.9 9.7 %collective-permute-start.10 = (f32[256,128]{1,0:T(8,128)S(1)}, f32[256,128]{1,0:T(8,128)S(1)}, u32[]{:S(2)}, u32[]{:S(2)}) collective-permute-start(f32[256,128]{1,0:T(8,128)S(1)} %bitcast_subtract_fusion.refs_2_), channel_id=1, source_target_pairs={{0,2},{2,4},{4,6},{6,8},{8,10},{10,12},{12,14},{14,0},{1,3},{3,5},... | collective-permute-start | bytes 393224 | tf_op jit(solution)/shard_map/ppermute | solution.py:60
  174.6 9.4 %collective-permute-start.12 = (f32[256,128]{1,0:T(8,128)S(1)}, f32[256,128]{1,0:T(8,128)S(1)}, u32[]{:S(2)}, u32[]{:S(2)}) collective-permute-start(f32[256,128]{1,0:T(8,128)S(1)} %collective-permute-done.10.refs_3_), channel_id=1, source_target_pairs={{0,2},{2,4},{4,6},{6,8},{8,10},{10,12},{12,14},{14,0},{1,3},{3,5},... | collective-permute-start | bytes 393224 | tf_op jit(solution)/shard_map/ppermute | solution.py:60
  177.9 30.9 %all-to-all-start.4 = ((f32[4,2,2,128,128]{4,3,2,1,0:T(8,128)}), f32[4,2,2,128,128]{4,3,2,1,0:T(8,128)S(1)}, u32[]{:S(2)}, u32[]{:S(2)}) async-start(f32[4,2,2,128,128]{4,3,2,1,0:T(8,128)} %bitcast.28), calls=%async_computation.4 | async-start | bytes 2097152 | tf_op jit(solution)/shard_map/all_to_all | solution.py:371
  184.0 9.1 %collective-permute-start.14 = (f32[256,128]{1,0:T(8,128)S(1)}, f32[256,128]{1,0:T(8,128)S(1)}, u32[]{:S(2)}, u32[]{:S(2)}) collective-permute-start(f32[256,128]{1,0:T(8,128)S(1)} %collective-permute-done.12.refs_5_), channel_id=1, source_target_pairs={{0,2},{2,4},{4,6},{6,8},{8,10},{10,12},{12,14},{14,0},{1,3},{3,5},... | collective-permute-start | bytes 393224 | tf_op jit(solution)/shard_map/ppermute | solution.py:60
  184.0 9.1 %collective-permute-start.15 = (f32[256,128]{1,0:T(8,128)S(1)}, f32[256,128]{1,0:T(8,128)S(1)}, u32[]{:S(2)}, u32[]{:S(2)}) collective-permute-start(f32[256,128]{1,0:T(8,128)S(1)} %collective-permute-done.13.refs_6_), channel_id=1, source_target_pairs={{0,14},{2,0},{4,2},{6,4},{8,6},{10,8},{12,10},{14,12},{1,15},{3,1}... | collective-permute-start | bytes 393224 | tf_op jit(solution)/shard_map/ppermute | solution.py:61
  193.2 9.6 %collective-permute-start.18 = (f32[192,128]{1,0:T(8,128)S(1)}, f32[192,128]{1,0:T(8,128)S(1)}, u32[]{:S(2)}, u32[]{:S(2)}) collective-permute-start(f32[192,128]{1,0:T(8,128)S(1)} %get-tuple-element.63), channel_id=1, source_target_pairs={{0,0},{1,8},{2,2},{3,10},{4,4},{5,12},{6,6},{7,14},{8,1},{9,9},{10... | collective-permute-start | bytes 294920 | tf_op jit(solution)/shard_map/ppermute | solution.py:385
  193.8 11.2 %collective-permute-start.19 = (f32[192,128]{1,0:T(8,128)S(1)}, f32[192,128]{1,0:T(8,128)S(1)}, u32[]{:S(2)}, u32[]{:S(2)}) collective-permute-start(f32[192,128]{1,0:T(8,128)S(1)} %get-tuple-element.64), channel_id=1, source_target_pairs={{0,8},{1,0},{2,10},{3,2},{4,12},{5,4},{6,14},{7,6},{8,9},{9,1},{10... | collective-permute-start | bytes 294920 | tf_op jit(solution)/shard_map/ppermute | solution.py:385
  199.6 9.2 %collective-permute-start.17 = (f32[128,128]{1,0:T(8,128)S(1)}, f32[128,128]{1,0:T(8,128)S(1)}, u32[]{:S(2)}, u32[]{:S(2)}) collective-permute-start(f32[128,128]{1,0:T(8,128)S(1)} %slice.63), channel_id=1, source_target_pairs={{0,14},{2,0},{4,2},{6,4},{8,6},{10,8},{12,10},{14,12},{1,15},{3,1}... | collective-permute-start | bytes 196616 | tf_op jit(solution)/shard_map/ppermute | solution.py:61
  210.0 18.0 %all-to-all-start.7 = ((f32[4,2,192,128]{3,2,1,0:T(8,128)}), f32[4,2,192,128]{3,2,1,0:T(8,128)}, u32[]{:S(2)}, u32[]{:S(2)}) async-start(f32[4,2,192,128]{3,2,1,0:T(8,128)} %broadcast_in_dim.16), calls=%async_computation.7 | async-start | bytes 1572864 | tf_op jit(solution)/shard_map/all_to_all | solution.py:70
  228.0 16.5 %all-to-all-start.6 = ((f32[4,2,96,128]{3,2,1,0:T(8,128)}), f32[4,2,96,128]{3,2,1,0:T(8,128)}, u32[]{:S(2)}, u32[]{:S(2)}) async-start(f32[4,2,96,128]{3,2,1,0:T(8,128)} %bitcast.100), calls=%async_computation.6 | async-start | bytes 786432 | tf_op jit(solution)/shard_map/all_to_all | solution.py:378
  244.5 22.4 %all-to-all-start.8 = ((f32[16,2,2,32,128]{4,3,2,1,0:T(8,128)}), f32[16,2,2,32,128]{4,3,2,1,0:T(8,128)S(1)}, u32[]{:S(2)}, u32[]{:S(2)}) async-start(f32[16,2,2,32,128]{4,3,2,1,0:T(8,128)} %bitcast.110), calls=%async_computation.8 | async-start | bytes 2097152 | tf_op jit(solution)/shard_map/all_to_all | solution.py:420
  267.1 9.8 %collective-permute-start.22 = (f32[2,32,128]{2,1,0:T(8,128)S(1)}, f32[2,32,128]{2,1,0:T(8,128)S(1)}, u32[]{:S(2)}, u32[]{:S(2)}) collective-permute-start(f32[2,32,128]{2,1,0:T(8,128)S(1)} %get-tuple-element.71), channel_id=1, source_target_pairs={{0,0},{1,1},{2,16},{3,17},{4,32},{5,33},{6,48},{7,49},{8,8},{9,9},... | collective-permute-start | bytes 98312 | tf_op jit(solution)/shard_map/ppermute | solution.py:425
  282.3 12.2 %all-to-all-start.9 = ((f32[4,10,32,128]{3,2,1,0:T(8,128)}), f32[4,10,32,128]{3,2,1,0:T(8,128)S(1)}, u32[]{:S(2)}, u32[]{:S(2)}) async-start(f32[4,10,32,128]{3,2,1,0:T(8,128)} %broadcast_in_dim.17), calls=%async_computation.9 | async-start | bytes 1310720 | tf_op jit(solution)/shard_map/all_to_all | solution.py:70
  (43 other events, 361.0 us)
Sparse Core Ops, SparseCore 0:
  29.3 59.0 all-gather.4
  130.4 87.1 all-gather.6
where the time goes:
time: 305 us; the launch traced here: 304 us
  waiting for transfers between devices  118 us (39%)
  starting transfers between devices  103 us (34%)
  Pallas kernels  38.3 us (13%)
  local copies, waits for them, and re-layouts  18.6 us (6%)
  between operations  15.3 us (5%)
  other arithmetic  10.8 us (4%)
    all_to_all x4, waiting for transfers between devices, spread(): lax.all_to_all(jnp.broadcast_to(value[None], (size,) + value.shape), axis...  41 us
    pallas_call x4, Pallas kernels, with_copies(): pl.pallas_call(kernel, out_shape=[jax.ShapeDtypeStruct(shape, jnp.float32...  28 us
    ppermute x8, waiting for transfers between devices, onward(): lax.ppermute(ahead, RING, ring_pairs(1))  27.4 us
    ppermute x8, starting transfers between devices, onward(): lax.ppermute(behind, RING, ring_pairs(-1))  25.4 us
    all_to_all x4, starting transfers between devices, spread(): lax.all_to_all(jnp.broadcast_to(value[None], (size,) + value.shape), axis...  21.1 us
    ppermute x2, waiting for transfers between devices, to_ring(): lax.ppermute(piece, LANE, lane_pairs(lambda h, l, c: (c, l, h ^ flip)))  15.7 us
    ppermute x4, starting transfers between devices, in_place(): lax.ppermute(piece, LANE, lane_pairs(lambda h, l, c: (c ^ flip, l, h)))  13.2 us
    pallas_call x1, Pallas kernels, leaf_cross(): pl.pallas_call(leaf_kernel, out_shape=jax.ShapeDtypeStruct((SIZE_X, SIZE_...  10.3 us
  transfers between devices with their start and end apart: 36, of which 21 were waited for; matrix products, arithmetic and copies ran while one was open for 7% of the time, Pallas kernels for 10%

commit v1 on v0

--- a/solution.py
+++ b/solution.py
@@ -108,14 +108,14 @@
 def outer_kernel(inverse, top, out, inverse_here, top_here, sems):
     order = [half * 8 + k for k in range(8) for half in range(2)]
     ready = fetched(
-        [top.at[:, 0:256, :]] + [inverse.at[at] for at in order],
-        [top_here.at[:, 0:256, :]] + [inverse_here.at[at] for at in order],
+        [top] + [inverse.at[at] for at in order],
+        [top_here] + [inverse_here.at[at] for at in order],
         sems,
     )
     ready(0)
     totals = [None, None]
     for k in range(8):
-        right = split(top_here[k, 0:256, :])
+        right = split(top_here[k])
         for half in range(2):
             left = split(ready(1 + k * 2 + half)[...])
             part = product(left, right)
@@ -125,16 +125,14 @@
 
 
 def cross_kernel(order, *refs):
-    sources, (top_out, leaf_out) = refs[:10], refs[10:12]
-    scratch, sems = refs[12:22], refs[22]
+    sources, (top_out, leaf_out) = refs[:11], refs[11:13]
+    scratch, sems = refs[13:24], refs[24]
     ready = fetched(sources, scratch, sems)
-    mine = ready(0)
+    top, mine = ready(0), ready(1)
     panels = split(
         jnp.concatenate(
             [
-                jnp.concatenate(
-                    [mine[zh, 0:256, :], mine[zh, 512:768, :], mine[zh, 768:1024, :]], axis=1
-                )
+                jnp.concatenate([top[zh], mine[zh, 256:512, :], mine[zh, 512:768, :]], axis=1)
                 for zh in range(SIZE_H)
             ],
             axis=0,
@@ -142,9 +140,9 @@
     )
     for at in range(8):
         if at < 7:
-            piece = ready(1 + at)[...]
+            piece = ready(2 + at)[...]
         else:
-            piece = jnp.concatenate([ready(8)[...], ready(9)[...]], axis=0)
+            piece = jnp.concatenate([ready(9)[...], ready(10)[...]], axis=0)
         part = product_t(split(piece), panels)
         top_out[order[at]] = part[:, :128]
         leaf_out[order[at], 0] = part[:, 128:256]
@@ -152,23 +150,23 @@
 
 
 def root_kernel(order, *refs):
-    sources, out = refs[:12], refs[12]
-    scratch, sems = refs[13:25], refs[25]
+    sources, out = refs[:11], refs[11]
+    scratch, sems = refs[12:23], refs[23]
     ready = fetched(sources, scratch, sems)
-    cols, last, inverse = ready(0), ready(1), ready(2)
+    cols, inverse = ready(0), ready(1)
     totals = [jnp.zeros((256, 256), jnp.float32) for _ in range(2)]
     for k in range(8):
-        root = split(jnp.concatenate([cols[k, 512:768, :], last[k]], axis=1))
+        root = split(jnp.concatenate([cols[k, 256:512, :], cols[k, 512:768, :]], axis=1))
         for half in range(2):
             totals[half] += product(split(inverse[half * 8 + k]), root)
     for at in range(8):
         if at < 7:
-            piece = ready(3 + at)[...]
+            piece = ready(2 + at)[...]
         else:
-            piece = jnp.concatenate([ready(10)[...], ready(11)[...]], axis=0)
+            piece = jnp.concatenate([ready(9)[...], ready(10)[...]], axis=0)
         place = order[at]
         parent = split(
-            jnp.concatenate([cols[place, 256:384, :], cols[place, 384:512, :]], axis=1)
+            jnp.concatenate([cols[place, 0:128, :], cols[place, 128:256, :]], axis=1)
         )
         for half in range(2):
             totals[half] += product(split(piece[half * 256 : (half + 1) * 256]), parent)
@@ -190,7 +188,7 @@
         else:
             piece = jnp.concatenate([ready(9)[...], ready(10)[...]], axis=0)
         place = order[at]
-        parent = jnp.concatenate([cols[place, 256:384, :], cols[place, 384:512, :]], axis=1)
+        parent = jnp.concatenate([cols[place, 0:128, :], cols[place, 128:256, :]], axis=1)
         total += product(split(piece), split(parent))
     for leaf in range(2):
         for sub in range(2):
@@ -310,56 +308,56 @@
             )
         return jnp.stack(in_order(core, got[0], got[1]))
 
-    block = to_ring(
-        jnp.concatenate(
-            [top, parent.reshape(2, 256, 128), root.reshape(2, 512, 128), top_pivots_inv[0]],
-            axis=1,
-        )
-    )
-    pivot_block = block[:, 1024:].reshape(256, 128)
-    first_cols = spread(block[:, :768], "y", SIZE_Y).reshape(8, 768, 128)
-    inverse, block = lax.optimization_barrier((root_inverse[0], block))
-    inverse = lax.all_gather(inverse, LANE, axis=0)
-
+    inverse = lax.all_gather(root_inverse[0], LANE, axis=0)
+
+    top_block = to_ring(jnp.concatenate([top, top_pivots_inv[0]], axis=1))
+    top_block, parent, root = lax.optimization_barrier((top_block, parent, root))
+    leaf_block = to_ring(
+        jnp.concatenate([parent.reshape(2, 256, 128), root.reshape(2, 512, 128)], axis=1)
+    )
+    pivot_block = top_block[:, 256:].reshape(256, 128)
+    top_block = top_block[:, :256]
+    top_cols = spread(top_block, "y", SIZE_Y).reshape(8, 256, 128)
     leaf = (weight * leaf_pivots_inv[0]).reshape(4, SIZE_X, 32, 128)
     leaf = jnp.sum(lax.all_to_all(jnp.moveaxis(leaf, 1, 0), "pole", 0, 0), axis=0)
-    first_cols, leaf = lax.optimization_barrier((first_cols, leaf))
+    top_cols, leaf, leaf_block = lax.optimization_barrier((top_cols, leaf, leaf_block))
+    inverse, leaf_block = lax.optimization_barrier((inverse, leaf_block))
+    leaf_cols = lax.all_gather(leaf_block, "y", axis=0).reshape(8, 768, 128)
 
     (outer,) = with_copies(
         outer_kernel,
         [(512, 128)],
         None,
         inverse,
-        first_cols,
+        top_cols,
         terms=512 * 2048 * 128,
         copies=17,
     )
-    last_cols = spread(block[:, 768:1024], "y", SIZE_Y).reshape(8, 256, 128)
     pieces = [outer]
     for step in range(3):
         pieces += onward(pieces, step)
-    pieces[5], pieces[6], leaves, last_cols = lax.optimization_barrier(
-        (pieces[5], pieces[6], leaves, last_cols)
-    )
+    pieces[5], pieces[6], leaves, leaf_cols = lax.optimization_barrier(
+        (pieces[5], pieces[6], leaves, leaf_cols)
+    )
+    panels = lax.all_gather(leaves, LANE, axis=0)
     pieces += onward(pieces, 3)
-    panels = lax.all_gather(leaves, LANE, axis=0)
     order = jnp.stack([column_of((place + d) % SIZE_Z) for d in (0, 7, 1, 6, 2, 5, 3, 4)])
 
     cross_top, cross_leaf = with_copies(
         cross_kernel,
         [(8, 128, 128), (8, 2, 128, 128)],
         order,
-        block,
+        top_block,
+        leaf_block,
         *pieces,
         terms=512 * 1024 * 384,
     )
-    cross_leaf, last_cols = lax.optimization_barrier((cross_leaf, last_cols))
+    cross_leaf, leaf_cols = lax.optimization_barrier((cross_leaf, leaf_cols))
     (leaf_root,) = with_copies(
         root_kernel,
         [(2, 512, 128)],
         order,
-        first_cols,
-        last_cols,
+        leaf_cols,
         inverse,
         *pieces,
         terms=512 * 3072 * 256,
@@ -406,7 +404,7 @@
         parent_kernel,
         [(2, 256, 128)],
         order,
-        first_cols,
+        leaf_cols,
         cross_leaf,
         *diag_pieces,
         terms=256 * 1024 * 256,

time: 305 us -> 289 us (0.948)
  waiting for transfers between devices: 118 us -> 101 us
  other arithmetic: 10.8 us -> 16 us
  local copies, waits for them, and re-layouts: 18.6 us -> 15 us
    all_to_all x4 -> x3, waiting for transfers between devices: 41 us -> 12.4 us  [spread(): lax.all_to_all(jnp.broadcast_to(value[None], (size,) + value.shape), axis...]
    ppermute x2 -> x4, starting transfers between devices: 0.79 us -> 11.3 us  [to_ring(): lax.ppermute(piece, LANE, lane_pairs(lambda h, l, c: (c, l, h ^ flip)))]
    ppermute x2 -> x4, waiting for transfers between devices: 15.7 us -> 26 us  [to_ring(): lax.ppermute(piece, LANE, lane_pairs(lambda h, l, c: (c, l, h ^ flip)))]
    all_to_all x4 -> x3, starting transfers between devices: 21.1 us -> 12.7 us  [spread(): lax.all_to_all(jnp.broadcast_to(value[None], (size,) + value.shape), axis...]
    ppermute x8, waiting for transfers between devices: 27.4 us -> 34.5 us  [onward(): lax.ppermute(ahead, RING, ring_pairs(1))]
    all_to_all x1, waiting for transfers between devices: 6.62 us -> 1.15 us  [body(): lax.all_to_all(jnp.moveaxis(leaf, 1, 0), 'pole', 0, 0)]
    ppermute x8, starting transfers between devices: 25.4 us -> 21.4 us  [onward(): lax.ppermute(behind, RING, ring_pairs(-1))]
    all_gather x1 -> x2, waiting for transfers between devices: 8.93 us -> 8.91 us  [the longest x1 5.51 us: body(): leaf_cols = lax.all_gather(leaf_block, 'y', axis=0).reshape(8, 768, 128)]
  transfers between devices with their start and end apart: 36 -> 38, of which waited for: 21 -> 21; matrix products, arithmetic and copies ran while one was open for 7% -> 9% of each run, Pallas kernels for 10% -> 13%
where the time goes in v1:
time: 289 us; the launch traced here: 287 us
  starting transfers between devices  103 us (36%)
  waiting for transfers between devices  101 us (35%)
  Pallas kernels  37.9 us (13%)
  other arithmetic  16 us (6%)
  local copies, waits for them, and re-layouts  15 us (5%)
  between operations  14.9 us (5%)
    ppermute x8, waiting for transfers between devices, onward(): lax.ppermute(ahead, RING, ring_pairs(1))  34.5 us
    pallas_call x4, Pallas kernels, with_copies(): pl.pallas_call(kernel, out_shape=[jax.ShapeDtypeStruct(shape, jnp.float32...  27.6 us
    ppermute x4, waiting for transfers between devices, to_ring(): lax.ppermute(piece, LANE, lane_pairs(lambda h, l, c: (c, l, h ^ flip)))  26 us
    ppermute x8, starting transfers between devices, onward(): lax.ppermute(behind, RING, ring_pairs(-1))  21.4 us
    ppermute x4, starting transfers between devices, in_place(): lax.ppermute(piece, LANE, lane_pairs(lambda h, l, c: (c ^ flip, l, h)))  14.1 us
    all_to_all x3, starting transfers between devices, spread(): lax.all_to_all(jnp.broadcast_to(value[None], (size,) + value.shape), axis...  12.7 us
    all_to_all x3, waiting for transfers between devices, spread(): lax.all_to_all(jnp.broadcast_to(value[None], (size,) + value.shape), axis...  12.4 us
    ppermute x4, starting transfers between devices, to_ring(): lax.ppermute(piece, LANE, lane_pairs(lambda h, l, c: (c, l, h ^ flip)))  11.3 us
  transfers between devices with their start and end apart: 38, of which 21 were waited for; matrix products, arithmetic and copies ran while one was open for 9% of the time, Pallas kernels for 13%

profile of v1, /device:TPU:24, one launch (start us, length us, event | category | flops | bytes accessed | tf_op | source)
XLA Modules:
  0.0 287.2 jit_solution(5407310443596318751)
XLA Ops:
  11.4 8.6 %collective-permute-start.1 = (f32[384,128]{1,0:T(8,128)S(1)}, f32[384,128]{1,0:T(8,128)S(1)}, u32[]{:S(2)}, u32[]{:S(2)}) collective-permute-start(f32[384,128]{1,0:T(8,128)S(1)} %get-tuple-element.70), channel_id=1, source_target_pairs={{0,1},{1,9},{2,3},{3,11},{4,5},{5,13},{6,7},{7,15},{8,0},{9,8},{10... | collective-permute-start | bytes 589832 | tf_op jit(solution)/shard_map/ppermute | solution.py:307
  22.3 4.3 %all-to-all-start.1 = ((f32[4,4,32,128]{3,2,1,0:T(8,128)}), f32[4,4,32,128]{3,2,1,0:T(8,128)S(1)}, u32[]{:S(2)}, u32[]{:S(2)}) async-start(f32[4,4,32,128]{3,2,1,0:T(8,128)} %copy.21), calls=%async_computation.1 | async-start | bytes 524288 | tf_op jit(solution)/shard_map/all_to_all | solution.py:322
  34.5 4.7 %all-to-all-start = ((f32[4,2,256,128]{3,2,1,0:T(8,128)}), f32[4,2,256,128]{3,2,1,0:T(8,128)}, u32[]{:S(2)}, u32[]{:S(2)}) async-start(f32[4,2,256,128]{3,2,1,0:T(8,128)} %broadcast_in_dim.12), calls=%async_computation | async-start | bytes 2097152 | tf_op jit(solution)/shard_map/all_to_all | solution.py:70
  39.9 26.0 %collective-permute-done.3 = f32[768,128]{1,0:T(8,128)S(1)} collective-permute-done((f32[768,128]{1,0:T(8,128)S(1)}, f32[768,128]{1,0:T(8,128)S(1)}, u32[]{:S(2)}, u32[]{:S(2)}) %collective-permute-start.3) | collective-permute-done | bytes 393248 | tf_op jit(solution)/shard_map/ppermute | solution.py:307
  70.4 6.8 %shard_map.137.refs_2_ = f32[512,128]{1,0:T(8,128)} custom-call(f32[16,256,256]{2,1,0:T(8,128)} %all-gather.6.cloned.1.call-done.inverse.refs_1_, f32[8,256,128]{2,1,0:T(8,128)} %bitcast.18.top), custom_call_target="tpu_custom_call" | custom-call | flops 805306368 | bytes 5505024 | tf_op jit(solution)/shard_map/pallas_call | solution.py:267
  80.4 6.6 %collective-permute-done.4.refs_3_ = f32[512,128]{1,0:T(8,128)S(1)} collective-permute-done((f32[512,128]{1,0:T(8,128)}, f32[512,128]{1,0:T(8,128)S(1)}, u32[]{:S(2)}, u32[]{:S(2)}) %collective-permute-start.4) | collective-permute-done | bytes 262176 | tf_op jit(solution)/shard_map/ppermute | solution.py:60
  90.3 5.7 %collective-permute-done.6.refs_5_ = f32[512,128]{1,0:T(8,128)S(1)} collective-permute-done((f32[512,128]{1,0:T(8,128)S(1)}, f32[512,128]{1,0:T(8,128)S(1)}, u32[]{:S(2)}, u32[]{:S(2)}) %collective-permute-start.6) | collective-permute-done | bytes 262176 | tf_op jit(solution)/shard_map/ppermute | solution.py:60
  104.2 5.5 %all-gather.8.cloned.1.call-done.refs_0_ = f32[8,768,128]{2,1,0:T(8,128)} async-done(((f32[2,768,128]{2,1,0:T(8,128)}), f32[8,768,128]{2,1,0:T(8,128)}) %all-gather.8.cloned.1.call-update) | async-done | bytes 3145744 | tf_op jit(solution)/shard_map/all_gather | solution.py:325
  117.1 6.5 %shard_map.138 = (f32[8,128,128]{2,1,0:T(8,128)}, f32[8,2,128,128]{3,2,1,0:T(8,128)}) custom-call(s32[8]{0:T(128)} %stack.74.order, f32[2,256,128]{2,1,0:T(8,128)} %copy-done.4, f32[2,768,128]{2,1,0:T(8,128)} %pad_maximum_fusion.refs_1_, f32[512,128]{1,0:T(8,128)} %shard_map.137.refs_2_, f32[512,128]{1,0:T(8,128)} %copy-done.10, f32[512,128]{1,0:T(8,128)} %copy-done.11, ...), custom_call_target="tpu_custom_call" | custom-call | flops 1207959552 | bytes 4718592 | tf_op jit(solution)/shard_map/pallas_call | solution.py:267
  123.6 6.4 %all-to-all-start.2 = ((f32[4,256,128]{2,1,0:T(8,128)}), f32[4,256,128]{2,1,0:T(8,128)}, u32[]{:S(2)}, u32[]{:S(2)}) async-start(f32[4,256,128]{2,1,0:T(8,128)} %bitcast.126), calls=%async_computation.2 | async-start | bytes 1048576 | tf_op jit(solution)/shard_map/all_to_all | solution.py:365
  130.0 8.6 %shard_map.139.root = f32[2,512,128]{2,1,0:T(8,128)} custom-call(s32[8]{0:T(128)} %stack.74.order, f32[8,768,128]{2,1,0:T(8,128)} %all-gather.8.cloned.1.call-done.refs_0_, f32[16,256,256]{2,1,0:T(8,128)} %all-gather.6.cloned.1.call-done.inverse.refs_1_, f32[512,128]{1,0:T(8,128)} %shard_map.137.refs_2_, f32[512,128]{1,0:T(8,128)} %copy-done.10, ...), custom_call_target="tpu_custom_call" | custom-call | flops 2415919104 | bytes 9961472 | tf_op jit(solution)/shard_map/pallas_call | solution.py:267
  152.0 6.3 %collective-permute-done.12.refs_3_ = f32[256,128]{1,0:T(8,128)S(1)} collective-permute-done((f32[256,128]{1,0:T(8,128)S(1)}, f32[256,128]{1,0:T(8,128)S(1)}, u32[]{:S(2)}, u32[]{:S(2)}) %collective-permute-start.12) | collective-permute-done | bytes 131104 | tf_op jit(solution)/shard_map/ppermute | solution.py:60
  161.6 4.8 %all-to-all-start.3 = ((f32[4,2,2,128,128]{4,3,2,1,0:T(8,128)}), f32[4,2,2,128,128]{4,3,2,1,0:T(8,128)}, u32[]{:S(2)}, u32[]{:S(2)}) async-start(f32[4,2,2,128,128]{4,3,2,1,0:T(8,128)} %bitcast.29), calls=%async_computation.3 | async-start | bytes 2097152 | tf_op jit(solution)/shard_map/all_to_all | solution.py:369
  171.0 5.7 %collective-permute-done.16.refs_7_ = f32[256,128]{1,0:T(8,128)S(1)} collective-permute-done((f32[256,128]{1,0:T(8,128)S(1)}, f32[256,128]{1,0:T(8,128)S(1)}, u32[]{:S(2)}, u32[]{:S(2)}) %collective-permute-start.16) | collective-permute-done | bytes 131104 | tf_op jit(solution)/shard_map/ppermute | solution.py:60
  177.5 6.6 %collective-permute-start.21 = (f32[192,128]{1,0:T(8,128)S(1)}, f32[192,128]{1,0:T(8,128)S(1)}, u32[]{:S(2)}, u32[]{:S(2)}) collective-permute-start(f32[192,128]{1,0:T(8,128)S(1)} %get-tuple-element.76), channel_id=1, source_target_pairs={{0,8},{1,0},{2,10},{3,2},{4,12},{5,4},{6,14},{7,6},{8,9},{9,1},{10... | collective-permute-start | bytes 294920 | tf_op jit(solution)/shard_map/ppermute | solution.py:383
  194.3 4.5 %all-to-all-start.6 = ((f32[4,2,192,128]{3,2,1,0:T(8,128)}), f32[4,2,192,128]{3,2,1,0:T(8,128)}, u32[]{:S(2)}, u32[]{:S(2)}) async-start(f32[4,2,192,128]{3,2,1,0:T(8,128)} %broadcast_in_dim.13), calls=%async_computation.6 | async-start | bytes 1572864 | tf_op jit(solution)/shard_map/all_to_all | solution.py:70
  198.8 5.7 %shard_map.140.parent = f32[2,256,128]{2,1,0:T(8,128)} custom-call(s32[8]{0:T(128)} %stack.74.order, f32[8,768,128]{2,1,0:T(8,128)} %all-gather.8.cloned.1.call-done.refs_0_, f32[4,2,2,128,128]{4,3,2,1,0:T(8,128)} %all-to-all-done.3.refs_1_, f32[256,128]{1,0:T(8,128)} %copy-done.7, f32[256,128]{1,0:T(8,128)} %copy-done.16, f32[256,128]{1,0:T(8,128)} %copy-done.17, ...), custom_call_target="tpu_custom_call" | custom-call | flops 402653184 | bytes 5505024 | tf_op jit(solution)/shard_map/pallas_call | solution.py:267
  207.2 5.2 %all-to-all-done.6 = f32[4,2,192,128]{3,2,1,0:T(8,128)} async-done(((f32[4,2,192,128]{3,2,1,0:T(8,128)}), f32[4,2,192,128]{3,2,1,0:T(8,128)}, u32[]{:S(2)}, u32[]{:S(2)}) %all-to-all-start.6) | async-done | bytes 786464 | tf_op jit(solution)/shard_map/all_to_all | solution.py:70
  218.6 10.3 %shard_map.141 = f32[4,4,2,2,32,128]{5,4,3,2,1,0:T(8,128)} custom-call(s32[1]{0:T(128)} %bitcast.49.core, f32[1]{0:T(128)} %copy.37.weight, f32[2,256,128]{2,1,0:T(8,128)} %shard_map.140.parent, f32[2,512,128]{2,1,0:T(8,128)} %shard_map.139.root, f32[16,4,384,128]{3,2,1,0:T(8,128)} %bitcast.107), custom_call_target="tpu_custom_call" | custom-call | flops 1207959552 | bytes 8126464 | tf_op jit(solution)/shard_map/pallas_call | solution.py:229
  228.9 7.9 %all-to-all-start.7 = ((f32[16,2,2,32,128]{4,3,2,1,0:T(8,128)}), f32[16,2,2,32,128]{4,3,2,1,0:T(8,128)S(1)}, u32[]{:S(2)}, u32[]{:S(2)}) async-start(f32[16,2,2,32,128]{4,3,2,1,0:T(8,128)} %bitcast.109), calls=%async_computation.7 | async-start | bytes 2097152 | tf_op jit(solution)/shard_map/all_to_all | solution.py:418
  238.5 6.1 %collective-permute-start.23 = (f32[96,128]{1,0:T(8,128)S(1)}, f32[96,128]{1,0:T(8,128)S(1)}, u32[]{:S(2)}, u32[]{:S(2)}) collective-permute-start(f32[96,128]{1,0:T(8,128)S(1)} %get-tuple-element.80), channel_id=1, source_target_pairs={{0,8},{1,0},{2,10},{3,2},{4,12},{5,4},{6,14},{7,6},{8,9},{9,1},{10... | collective-permute-start | bytes 147464 | tf_op jit(solution)/shard_map/ppermute | solution.py:383
  246.6 4.9 %all-to-all-done.7 = f32[16,2,2,32,128]{4,3,2,1,0:T(8,128)S(1)} async-done(((f32[16,2,2,32,128]{4,3,2,1,0:T(8,128)}), f32[16,2,2,32,128]{4,3,2,1,0:T(8,128)S(1)}, u32[]{:S(2)}, u32[]{:S(2)}) %all-to-all-start.7) | async-done | bytes 1048608 | tf_op jit(solution)/shard_map/all_to_all | solution.py:418
  251.6 6.3 %collective-permute-start.24 = (f32[2,32,128]{2,1,0:T(8,128)S(1)}, f32[2,32,128]{2,1,0:T(8,128)S(1)}, u32[]{:S(2)}, u32[]{:S(2)}) collective-permute-start(f32[2,32,128]{2,1,0:T(8,128)S(1)} %get-tuple-element.83), channel_id=1, source_target_pairs={{0,0},{1,1},{2,16},{3,17},{4,32},{5,33},{6,48},{7,49},{8,8},{9,9},... | collective-permute-start | bytes 98312 | tf_op jit(solution)/shard_map/ppermute | solution.py:423
  271.3 7.2 %all-to-all-done.8 = f32[4,10,32,128]{3,2,1,0:T(8,128)S(1)} async-done(((f32[4,10,32,128]{3,2,1,0:T(8,128)}), f32[4,10,32,128]{3,2,1,0:T(8,128)S(1)}, u32[]{:S(2)}, u32[]{:S(2)}) %all-to-all-start.8) | async-done | bytes 655392 | tf_op jit(solution)/shard_map/all_to_all | solution.py:70
  (165 shorter events, 101.0 us)
Async XLA Ops:
  7.2 63.1 %all-gather.6.cloned.1.call-start = ((), (), s32[]{:S(2)}) async-start(), calls=%async_computation.9 | async-start | bytes 4456448 | tf_op jit(solution)/shard_map/all_gather | solution.py:311
  10.7 18.8 %collective-permute-start = (f32[384,128]{1,0:T(8,128)S(1)}, f32[384,128]{1,0:T(8,128)S(1)}, u32[]{:S(2)}, u32[]{:S(2)}) collective-permute-start(f32[384,128]{1,0:T(8,128)S(1)} %get-tuple-element.69), channel_id=1, source_target_pairs={{0,0},{1,8},{2,2},{3,10},{4,4},{5,12},{6,6},{7,14},{8,1},{9,9},{10... | collective-permute-start | bytes 589832 | tf_op jit(solution)/shard_map/ppermute | solution.py:307
  11.4 18.2 %collective-permute-start.1 = (f32[384,128]{1,0:T(8,128)S(1)}, f32[384,128]{1,0:T(8,128)S(1)}, u32[]{:S(2)}, u32[]{:S(2)}) collective-permute-start(f32[384,128]{1,0:T(8,128)S(1)} %get-tuple-element.70), channel_id=1, source_target_pairs={{0,1},{1,9},{2,3},{3,11},{4,5},{5,13},{6,7},{7,15},{8,0},{9,8},{10... | collective-permute-start | bytes 589832 | tf_op jit(solution)/shard_map/ppermute | solution.py:307
  22.3 11.1 %all-to-all-start.1 = ((f32[4,4,32,128]{3,2,1,0:T(8,128)}), f32[4,4,32,128]{3,2,1,0:T(8,128)S(1)}, u32[]{:S(2)}, u32[]{:S(2)}) async-start(f32[4,4,32,128]{3,2,1,0:T(8,128)} %copy.21), calls=%async_computation.1 | async-start | bytes 524288 | tf_op jit(solution)/shard_map/all_to_all | solution.py:322
  30.3 9.6 %collective-permute-start.2 = (f32[768,128]{1,0:T(8,128)S(1)}, f32[768,128]{1,0:T(8,128)S(1)}, u32[]{:S(2)}, u32[]{:S(2)}) collective-permute-start(f32[768,128]{1,0:T(8,128)S(1)} %get-tuple-element.61), channel_id=1, source_target_pairs={{0,0},{1,8},{2,2},{3,10},{4,4},{5,12},{6,6},{7,14},{8,1},{9,9},{10... | collective-permute-start | bytes 1179656 | tf_op jit(solution)/shard_map/ppermute | solution.py:307
  31.0 34.9 %collective-permute-start.3 = (f32[768,128]{1,0:T(8,128)S(1)}, f32[768,128]{1,0:T(8,128)S(1)}, u32[]{:S(2)}, u32[]{:S(2)}) collective-permute-start(f32[768,128]{1,0:T(8,128)S(1)} %get-tuple-element.62), channel_id=1, source_target_pairs={{0,1},{1,9},{2,3},{3,11},{4,5},{5,13},{6,7},{7,15},{8,0},{9,8},{10... | collective-permute-start | bytes 1179656 | tf_op jit(solution)/shard_map/ppermute | solution.py:307
  34.5 32.4 %all-to-all-start = ((f32[4,2,256,128]{3,2,1,0:T(8,128)}), f32[4,2,256,128]{3,2,1,0:T(8,128)}, u32[]{:S(2)}, u32[]{:S(2)}) async-start(f32[4,2,256,128]{3,2,1,0:T(8,128)} %broadcast_in_dim.12), calls=%async_computation | async-start | bytes 2097152 | tf_op jit(solution)/shard_map/all_to_all | solution.py:70
  39.2 70.5 %all-gather.8.cloned.1.call-start = ((), (), s32[]{:S(2)}) async-start(), calls=%async_computation.10 | async-start | bytes 3932160 | tf_op jit(solution)/shard_map/all_gather | solution.py:325
  70.3 148.3 %all-gather.10.cloned.1.call-start = ((), (), s32[]{:S(2)}) async-start(), calls=%async_computation.11 | async-start | bytes 13369344 | tf_op jit(solution)/shard_map/all_gather | solution.py:342
  77.1 10.0 %collective-permute-start.4 = (f32[512,128]{1,0:T(8,128)}, f32[512,128]{1,0:T(8,128)S(1)}, u32[]{:S(2)}, u32[]{:S(2)}) collective-permute-start(f32[512,128]{1,0:T(8,128)} %shard_map.137.refs_2_), channel_id=1, source_target_pairs={{0,2},{2,4},{4,6},{6,8},{8,10},{10,12},{12,14},{14,0},{1,3},{3,5},... | collective-permute-start | bytes 786440 | tf_op jit(solution)/shard_map/ppermute | solution.py:60
  123.6 15.0 %all-to-all-start.2 = ((f32[4,256,128]{2,1,0:T(8,128)}), f32[4,256,128]{2,1,0:T(8,128)}, u32[]{:S(2)}, u32[]{:S(2)}) async-start(f32[4,256,128]{2,1,0:T(8,128)} %bitcast.126), calls=%async_computation.2 | async-start | bytes 1048576 | tf_op jit(solution)/shard_map/all_to_all | solution.py:365
  142.8 18.8 %all-to-all-start.4 = ((f32[4,2,192,128]{3,2,1,0:T(8,128)}), f32[4,2,192,128]{3,2,1,0:T(8,128)S(1)}, u32[]{:S(2)}, u32[]{:S(2)}) async-start(f32[4,2,192,128]{3,2,1,0:T(8,128)} %copy.22), calls=%async_computation.4 | async-start | bytes 1572864 | tf_op jit(solution)/shard_map/all_to_all | solution.py:376
  148.7 9.7 %collective-permute-start.12 = (f32[256,128]{1,0:T(8,128)S(1)}, f32[256,128]{1,0:T(8,128)S(1)}, u32[]{:S(2)}, u32[]{:S(2)}) collective-permute-start(f32[256,128]{1,0:T(8,128)S(1)} %bitcast_subtract_fusion.refs_2_), channel_id=1, source_target_pairs={{0,2},{2,4},{4,6},{6,8},{8,10},{10,12},{12,14},{14,0},{1,3},{3,5},... | collective-permute-start | bytes 393224 | tf_op jit(solution)/shard_map/ppermute | solution.py:60
  158.3 9.3 %collective-permute-start.14 = (f32[256,128]{1,0:T(8,128)S(1)}, f32[256,128]{1,0:T(8,128)S(1)}, u32[]{:S(2)}, u32[]{:S(2)}) collective-permute-start(f32[256,128]{1,0:T(8,128)S(1)} %collective-permute-done.12.refs_3_), channel_id=1, source_target_pairs={{0,2},{2,4},{4,6},{6,8},{8,10},{10,12},{12,14},{14,0},{1,3},{3,5},... | collective-permute-start | bytes 393224 | tf_op jit(solution)/shard_map/ppermute | solution.py:60
  161.6 31.6 %all-to-all-start.3 = ((f32[4,2,2,128,128]{4,3,2,1,0:T(8,128)}), f32[4,2,2,128,128]{4,3,2,1,0:T(8,128)}, u32[]{:S(2)}, u32[]{:S(2)}) async-start(f32[4,2,2,128,128]{4,3,2,1,0:T(8,128)} %bitcast.29), calls=%async_computation.3 | async-start | bytes 2097152 | tf_op jit(solution)/shard_map/all_to_all | solution.py:369
  167.7 9.1 %collective-permute-start.16 = (f32[256,128]{1,0:T(8,128)S(1)}, f32[256,128]{1,0:T(8,128)S(1)}, u32[]{:S(2)}, u32[]{:S(2)}) collective-permute-start(f32[256,128]{1,0:T(8,128)S(1)} %collective-permute-done.14.refs_5_), channel_id=1, source_target_pairs={{0,2},{2,4},{4,6},{6,8},{8,10},{10,12},{12,14},{14,0},{1,3},{3,5},... | collective-permute-start | bytes 393224 | tf_op jit(solution)/shard_map/ppermute | solution.py:60
  176.8 10.5 %collective-permute-start.20 = (f32[192,128]{1,0:T(8,128)S(1)}, f32[192,128]{1,0:T(8,128)S(1)}, u32[]{:S(2)}, u32[]{:S(2)}) collective-permute-start(f32[192,128]{1,0:T(8,128)S(1)} %get-tuple-element.75), channel_id=1, source_target_pairs={{0,0},{1,8},{2,2},{3,10},{4,4},{5,12},{6,6},{7,14},{8,1},{9,9},{10... | collective-permute-start | bytes 294920 | tf_op jit(solution)/shard_map/ppermute | solution.py:383
  177.5 12.3 %collective-permute-start.21 = (f32[192,128]{1,0:T(8,128)S(1)}, f32[192,128]{1,0:T(8,128)S(1)}, u32[]{:S(2)}, u32[]{:S(2)}) collective-permute-start(f32[192,128]{1,0:T(8,128)S(1)} %get-tuple-element.76), channel_id=1, source_target_pairs={{0,8},{1,0},{2,10},{3,2},{4,12},{5,4},{6,14},{7,6},{8,9},{9,1},{10... | collective-permute-start | bytes 294920 | tf_op jit(solution)/shard_map/ppermute | solution.py:383
  184.1 9.2 %collective-permute-start.19 = (f32[128,128]{1,0:T(8,128)S(1)}, f32[128,128]{1,0:T(8,128)S(1)}, u32[]{:S(2)}, u32[]{:S(2)}) collective-permute-start(f32[128,128]{1,0:T(8,128)S(1)} %slice.59), channel_id=1, source_target_pairs={{0,14},{2,0},{4,2},{6,4},{8,6},{10,8},{12,10},{14,12},{1,15},{3,1}... | collective-permute-start | bytes 196616 | tf_op jit(solution)/shard_map/ppermute | solution.py:61
  194.3 18.1 %all-to-all-start.6 = ((f32[4,2,192,128]{3,2,1,0:T(8,128)}), f32[4,2,192,128]{3,2,1,0:T(8,128)}, u32[]{:S(2)}, u32[]{:S(2)}) async-start(f32[4,2,192,128]{3,2,1,0:T(8,128)} %broadcast_in_dim.13), calls=%async_computation.6 | async-start | bytes 1572864 | tf_op jit(solution)/shard_map/all_to_all | solution.py:70
  212.4 16.5 %all-to-all-start.5 = ((f32[4,2,96,128]{3,2,1,0:T(8,128)}), f32[4,2,96,128]{3,2,1,0:T(8,128)}, u32[]{:S(2)}, u32[]{:S(2)}) async-start(f32[4,2,96,128]{3,2,1,0:T(8,128)} %bitcast.101), calls=%async_computation.5 | async-start | bytes 786432 | tf_op jit(solution)/shard_map/all_to_all | solution.py:376
  228.9 22.6 %all-to-all-start.7 = ((f32[16,2,2,32,128]{4,3,2,1,0:T(8,128)}), f32[16,2,2,32,128]{4,3,2,1,0:T(8,128)S(1)}, u32[]{:S(2)}, u32[]{:S(2)}) async-start(f32[16,2,2,32,128]{4,3,2,1,0:T(8,128)} %bitcast.109), calls=%async_computation.7 | async-start | bytes 2097152 | tf_op jit(solution)/shard_map/all_to_all | solution.py:418
  251.6 9.8 %collective-permute-start.24 = (f32[2,32,128]{2,1,0:T(8,128)S(1)}, f32[2,32,128]{2,1,0:T(8,128)S(1)}, u32[]{:S(2)}, u32[]{:S(2)}) collective-permute-start(f32[2,32,128]{2,1,0:T(8,128)S(1)} %get-tuple-element.83), channel_id=1, source_target_pairs={{0,0},{1,1},{2,16},{3,17},{4,32},{5,33},{6,48},{7,49},{8,8},{9,9},... | collective-permute-start | bytes 98312 | tf_op jit(solution)/shard_map/ppermute | solution.py:423
  266.2 12.2 %all-to-all-start.8 = ((f32[4,10,32,128]{3,2,1,0:T(8,128)}), f32[4,10,32,128]{3,2,1,0:T(8,128)S(1)}, u32[]{:S(2)}, u32[]{:S(2)}) async-start(f32[4,10,32,128]{3,2,1,0:T(8,128)} %broadcast_in_dim.14), calls=%async_computation.8 | async-start | bytes 1310720 | tf_op jit(solution)/shard_map/all_to_all | solution.py:70
  (36 other events, 437.4 us)
Sparse Core Ops, SparseCore 0:
  9.8 60.4 all-gather.5
  72.1 37.5 all-gather.7
  111.6 91.7 all-gather.9

commit v2 on v1

--- a/solution.py
+++ b/solution.py
@@ -336,11 +336,9 @@
     pieces = [outer]
     for step in range(3):
         pieces += onward(pieces, step)
-    pieces[5], pieces[6], leaves, leaf_cols = lax.optimization_barrier(
-        (pieces[5], pieces[6], leaves, leaf_cols)
-    )
+    pieces += onward(pieces, 3)
+    pieces[7], pieces[8], leaves = lax.optimization_barrier((pieces[7], pieces[8], leaves))
     panels = lax.all_gather(leaves, LANE, axis=0)
-    pieces += onward(pieces, 3)
     order = jnp.stack([column_of((place + d) % SIZE_Z) for d in (0, 7, 1, 6, 2, 5, 3, 4)])
 
     cross_top, cross_leaf = with_copies(
@@ -391,7 +389,7 @@
     diag_pieces = [top_diag]
     for step in range(3):
         diag_pieces += onward(diag_pieces, step)
-    early = summed([outer, leaf_root[0], leaf_root[1]])
+    early = summed([outer, leaf_root[0], leaf_root[1], top_diag])
     diag_pieces[5], diag_pieces[6], early = lax.optimization_barrier(
         (diag_pieces[5], diag_pieces[6], early)
     )
@@ -410,7 +408,7 @@
         terms=256 * 1024 * 256,
     )
     early = everywhere(early)
-    late = summed([top_diag, leaf_parent[0], leaf_parent[1]])
+    late = summed([leaf_parent[0], leaf_parent[1]])
 
     cross = leaf_cross(core.reshape(1), pole_weights, leaf_parent, leaf_root, panels)
     cross, early = lax.optimization_barrier((cross, early))
@@ -422,13 +420,13 @@
         piece = lax.dynamic_index_in_dim(cross, core ^ flip, 0, keepdims=False)
         got.append(lax.ppermute(piece, PLANE, plane_pairs(flip)))
     cross = jnp.concatenate(in_order(core, got[0], got[1]), axis=0)
-    ends = everywhere(jnp.concatenate([late.reshape(6, 32, 128), leaf - cross], axis=0))
+    ends = everywhere(jnp.concatenate([late.reshape(4, 32, 128), leaf - cross], axis=0))
     outer_dens = early[:, :256]
-    rootward_dens = early[:, 256:].reshape(4, 256, 128)
-    leaf_dens = ends[6:]
-    late = jnp.moveaxis(ends[:6].reshape(2, 3, SIZE_X, 32, 128), 2, 1).reshape(2, 384, 128)
-    top_dens = late[:, :128]
-    parent_dens = late[:, 128:].reshape(4, 128, 128)
+    rootward_dens = early[:, 256:768].reshape(4, 256, 128)
+    top_dens = early[:, 768:]
+    leaf_dens = ends[4:]
+    parent_dens = jnp.moveaxis(ends[:4].reshape(2, 2, SIZE_X, 32, 128), 2, 1)
+    parent_dens = parent_dens.reshape(4, 128, 128)
     return (top_dens, outer_dens, leaf_dens, parent_dens, rootward_dens)
 
 

time: 289 us -> 283 us (0.979)
  waiting for transfers between devices: 101 us -> 96.7 us
    all_gather x1, waiting for transfers between devices: 5.51 us -> 0.01 us  [body(): leaf_cols = lax.all_gather(leaf_block, 'y', axis=0).reshape(8, 768, 128)]
    ppermute x8, starting transfers between devices: 21.4 us -> 25 us  [onward(): lax.ppermute(behind, RING, ring_pairs(-1))]
  transfers between devices with their start and end apart: 38 -> 38, of which waited for: 21 -> 20; matrix products, arithmetic and copies ran while one was open for 9% -> 9% of each run, Pallas kernels for 13% -> 13%
where the time goes in v2:
time: 283 us; the launch traced here: 282 us
  starting transfers between devices  101 us (36%)
  waiting for transfers between devices  96.7 us (34%)
  Pallas kernels  38 us (13%)
  local copies, waits for them, and re-layouts  16.4 us (6%)
  between operations  15.3 us (5%)
  other arithmetic  14.4 us (5%)
    ppermute x8, waiting for transfers between devices, onward(): lax.ppermute(ahead, RING, ring_pairs(1))  32.9 us
    pallas_call x4, Pallas kernels, with_copies(): pl.pallas_call(kernel, out_shape=[jax.ShapeDtypeStruct(shape, jnp.float32...  27.7 us
    ppermute x4, waiting for transfers between devices, to_ring(): lax.ppermute(piece, LANE, lane_pairs(lambda h, l, c: (c, l, h ^ flip)))  26 us
    ppermute x8, starting transfers between devices, onward(): lax.ppermute(behind, RING, ring_pairs(-1))  25 us
    all_to_all x3, starting transfers between devices, spread(): lax.all_to_all(jnp.broadcast_to(value[None], (size,) + value.shape), axis...  13.1 us
    all_to_all x3, waiting for transfers between devices, spread(): lax.all_to_all(jnp.broadcast_to(value[None], (size,) + value.shape), axis...  13 us
    ppermute x4, starting transfers between devices, to_ring(): lax.ppermute(piece, LANE, lane_pairs(lambda h, l, c: (c, l, h ^ flip)))  11.3 us
    ppermute x4, starting transfers between devices, in_place(): lax.ppermute(piece, LANE, lane_pairs(lambda h, l, c: (c ^ flip, l, h)))  11.2 us
  transfers between devices with their start and end apart: 38, of which 20 were waited for; matrix products, arithmetic and copies ran while one was open for 9% of the time, Pallas kernels for 13%

profile of v2, /device:TPU:24, one launch (start us, length us, event | category | flops | bytes accessed | tf_op | source)
XLA Modules:
  0.0 281.5 jit_solution(8497402971349711005)
XLA Ops:
  11.4 8.6 %collective-permute-start.1 = (f32[384,128]{1,0:T(8,128)S(1)}, f32[384,128]{1,0:T(8,128)S(1)}, u32[]{:S(2)}, u32[]{:S(2)}) collective-permute-start(f32[384,128]{1,0:T(8,128)S(1)} %get-tuple-element.70), channel_id=1, source_target_pairs={{0,1},{1,9},{2,3},{3,11},{4,5},{5,13},{6,7},{7,15},{8,0},{9,8},{10... | collective-permute-start | bytes 589832 | tf_op jit(solution)/shard_map/ppermute | solution.py:307
  34.5 4.7 %all-to-all-start = ((f32[4,2,256,128]{3,2,1,0:T(8,128)}), f32[4,2,256,128]{3,2,1,0:T(8,128)}, u32[]{:S(2)}, u32[]{:S(2)}) async-start(f32[4,2,256,128]{3,2,1,0:T(8,128)} %broadcast_in_dim.12), calls=%async_computation | async-start | bytes 2097152 | tf_op jit(solution)/shard_map/all_to_all | solution.py:70
  39.9 26.0 %collective-permute-done.3 = f32[768,128]{1,0:T(8,128)S(1)} collective-permute-done((f32[768,128]{1,0:T(8,128)S(1)}, f32[768,128]{1,0:T(8,128)S(1)}, u32[]{:S(2)}, u32[]{:S(2)}) %collective-permute-start.3) | collective-permute-done | bytes 393248 | tf_op jit(solution)/shard_map/ppermute | solution.py:307
  70.4 6.8 %shard_map.137.refs_2_ = f32[512,128]{1,0:T(8,128)} custom-call(f32[16,256,256]{2,1,0:T(8,128)} %all-gather.6.cloned.1.call-done.inverse.refs_1_, f32[8,256,128]{2,1,0:T(8,128)} %bitcast.18.top), custom_call_target="tpu_custom_call" | custom-call | flops 805306368 | bytes 5505024 | tf_op jit(solution)/shard_map/pallas_call | solution.py:267
  80.4 6.6 %collective-permute-done.4.refs_3_ = f32[512,128]{1,0:T(8,128)S(1)} collective-permute-done((f32[512,128]{1,0:T(8,128)}, f32[512,128]{1,0:T(8,128)S(1)}, u32[]{:S(2)}, u32[]{:S(2)}) %collective-permute-start.4) | collective-permute-done | bytes 262176 | tf_op jit(solution)/shard_map/ppermute | solution.py:60
  90.3 5.7 %collective-permute-done.6.refs_5_ = f32[512,128]{1,0:T(8,128)S(1)} collective-permute-done((f32[512,128]{1,0:T(8,128)S(1)}, f32[512,128]{1,0:T(8,128)S(1)}, u32[]{:S(2)}, u32[]{:S(2)}) %collective-permute-start.6) | collective-permute-done | bytes 262176 | tf_op jit(solution)/shard_map/ppermute | solution.py:60
  99.4 4.8 %collective-permute-done.8.refs_7_ = f32[512,128]{1,0:T(8,128)S(1)} collective-permute-done((f32[512,128]{1,0:T(8,128)S(1)}, f32[512,128]{1,0:T(8,128)S(1)}, u32[]{:S(2)}, u32[]{:S(2)}) %collective-permute-start.8) | collective-permute-done | bytes 262176 | tf_op jit(solution)/shard_map/ppermute | solution.py:60
  112.8 6.5 %shard_map.138 = (f32[8,128,128]{2,1,0:T(8,128)}, f32[8,2,128,128]{3,2,1,0:T(8,128)}) custom-call(s32[8]{0:T(128)} %stack.71.order, f32[2,256,128]{2,1,0:T(8,128)} %copy-done.4, f32[2,768,128]{2,1,0:T(8,128)} %pad_maximum_fusion.refs_1_, f32[512,128]{1,0:T(8,128)} %shard_map.137.refs_2_, f32[512,128]{1,0:T(8,128)} %copy-done.10, f32[512,128]{1,0:T(8,128)} %copy-done.11, ...), custom_call_target="tpu_custom_call" | custom-call | flops 1207959552 | bytes 4718592 | tf_op jit(solution)/shard_map/pallas_call | solution.py:267
  119.3 4.5 %all-to-all-start.2 = ((f32[4,256,128]{2,1,0:T(8,128)}), f32[4,256,128]{2,1,0:T(8,128)}, u32[]{:S(2)}, u32[]{:S(2)}) async-start(f32[4,256,128]{2,1,0:T(8,128)} %bitcast.122), calls=%async_computation.2 | async-start | bytes 1048576 | tf_op jit(solution)/shard_map/all_to_all | solution.py:363
  123.8 8.7 %shard_map.139.root = f32[2,512,128]{2,1,0:T(8,128)} custom-call(s32[8]{0:T(128)} %stack.71.order, f32[8,768,128]{2,1,0:T(8,128)} %all-gather.8.cloned.1.call-done.refs_0_, f32[16,256,256]{2,1,0:T(8,128)} %all-gather.6.cloned.1.call-done.inverse.refs_1_, f32[512,128]{1,0:T(8,128)} %shard_map.137.refs_2_, f32[512,128]{1,0:T(8,128)} %copy-done.10, ...), custom_call_target="tpu_custom_call" | custom-call | flops 2415919104 | bytes 9961472 | tf_op jit(solution)/shard_map/pallas_call | solution.py:267
  145.7 5.8 %collective-permute-done.12.refs_3_ = f32[256,128]{1,0:T(8,128)S(1)} collective-permute-done((f32[256,128]{1,0:T(8,128)S(1)}, f32[256,128]{1,0:T(8,128)S(1)}, u32[]{:S(2)}, u32[]{:S(2)}) %collective-permute-start.12) | collective-permute-done | bytes 131104 | tf_op jit(solution)/shard_map/ppermute | solution.py:60
  154.9 4.9 %all-to-all-start.3 = ((f32[4,2,2,128,128]{4,3,2,1,0:T(8,128)}), f32[4,2,2,128,128]{4,3,2,1,0:T(8,128)}, u32[]{:S(2)}, u32[]{:S(2)}) async-start(f32[4,2,2,128,128]{4,3,2,1,0:T(8,128)} %bitcast.29), calls=%async_computation.3 | async-start | bytes 2097152 | tf_op jit(solution)/shard_map/all_to_all | solution.py:367
  164.5 5.4 %collective-permute-done.16.refs_7_ = f32[256,128]{1,0:T(8,128)S(1)} collective-permute-done((f32[256,128]{1,0:T(8,128)S(1)}, f32[256,128]{1,0:T(8,128)S(1)}, u32[]{:S(2)}, u32[]{:S(2)}) %collective-permute-start.16) | collective-permute-done | bytes 131104 | tf_op jit(solution)/shard_map/ppermute | solution.py:60
  170.6 4.3 %collective-permute-start.21 = (f32[224,128]{1,0:T(8,128)S(1)}, f32[224,128]{1,0:T(8,128)S(1)}, u32[]{:S(2)}, u32[]{:S(2)}) collective-permute-start(f32[224,128]{1,0:T(8,128)S(1)} %get-tuple-element.76), channel_id=1, source_target_pairs={{0,8},{1,0},{2,10},{3,2},{4,12},{5,4},{6,14},{7,6},{8,9},{9,1},{10... | collective-permute-start | bytes 344072 | tf_op jit(solution)/shard_map/ppermute | solution.py:381
  187.6 5.0 %all-to-all-start.5 = ((f32[4,2,224,128]{3,2,1,0:T(8,128)}), f32[4,2,224,128]{3,2,1,0:T(8,128)}, u32[]{:S(2)}, u32[]{:S(2)}) async-start(f32[4,2,224,128]{3,2,1,0:T(8,128)} %broadcast_in_dim.13), calls=%async_computation.5 | async-start | bytes 1835008 | tf_op jit(solution)/shard_map/all_to_all | solution.py:70
  192.6 5.7 %shard_map.140.parent = f32[2,256,128]{2,1,0:T(8,128)} custom-call(s32[8]{0:T(128)} %stack.71.order, f32[8,768,128]{2,1,0:T(8,128)} %all-gather.8.cloned.1.call-done.refs_0_, f32[4,2,2,128,128]{4,3,2,1,0:T(8,128)} %all-to-all-done.3.refs_1_, f32[256,128]{1,0:T(8,128)} %copy-done.7, f32[256,128]{1,0:T(8,128)} %copy-done.16, f32[256,128]{1,0:T(8,128)} %copy-done.17, ...), custom_call_target="tpu_custom_call" | custom-call | flops 402653184 | bytes 5505024 | tf_op jit(solution)/shard_map/pallas_call | solution.py:267
  200.0 7.1 %all-to-all-done.5 = f32[4,2,224,128]{3,2,1,0:T(8,128)} async-done(((f32[4,2,224,128]{3,2,1,0:T(8,128)}), f32[4,2,224,128]{3,2,1,0:T(8,128)}, u32[]{:S(2)}, u32[]{:S(2)}) %all-to-all-start.5) | async-done | bytes 917536 | tf_op jit(solution)/shard_map/all_to_all | solution.py:70
  213.4 10.3 %shard_map.141 = f32[4,4,2,2,32,128]{5,4,3,2,1,0:T(8,128)} custom-call(s32[1]{0:T(128)} %bitcast.core, f32[1]{0:T(128)} %copy.37.weight, f32[2,256,128]{2,1,0:T(8,128)} %shard_map.140.parent, f32[2,512,128]{2,1,0:T(8,128)} %shard_map.139.root, f32[16,4,384,128]{3,2,1,0:T(8,128)} %bitcast.105), custom_call_target="tpu_custom_call" | custom-call | flops 1207959552 | bytes 8126464 | tf_op jit(solution)/shard_map/pallas_call | solution.py:229
  223.7 8.0 %all-to-all-start.7 = ((f32[16,2,2,32,128]{4,3,2,1,0:T(8,128)}), f32[16,2,2,32,128]{4,3,2,1,0:T(8,128)S(1)}, u32[]{:S(2)}, u32[]{:S(2)}) async-start(f32[16,2,2,32,128]{4,3,2,1,0:T(8,128)} %bitcast.107), calls=%async_computation.7 | async-start | bytes 2097152 | tf_op jit(solution)/shard_map/all_to_all | solution.py:416
  233.4 5.5 %collective-permute-start.23 = (f32[64,128]{1,0:T(8,128)S(1)}, f32[64,128]{1,0:T(8,128)S(1)}, u32[]{:S(2)}, u32[]{:S(2)}) collective-permute-start(f32[64,128]{1,0:T(8,128)S(1)} %get-tuple-element.80), channel_id=1, source_target_pairs={{0,8},{1,0},{2,10},{3,2},{4,12},{5,4},{6,14},{7,6},{8,9},{9,1},{10... | collective-permute-start | bytes 98312 | tf_op jit(solution)/shard_map/ppermute | solution.py:381
  240.5 5.3 %all-to-all-done.7 = f32[16,2,2,32,128]{4,3,2,1,0:T(8,128)S(1)} async-done(((f32[16,2,2,32,128]{4,3,2,1,0:T(8,128)}), f32[16,2,2,32,128]{4,3,2,1,0:T(8,128)S(1)}, u32[]{:S(2)}, u32[]{:S(2)}) %all-to-all-start.7) | async-done | bytes 1048608 | tf_op jit(solution)/shard_map/all_to_all | solution.py:416
  245.9 7.8 %collective-permute-start.24 = (f32[2,32,128]{2,1,0:T(8,128)S(1)}, f32[2,32,128]{2,1,0:T(8,128)S(1)}, u32[]{:S(2)}, u32[]{:S(2)}) collective-permute-start(f32[2,32,128]{2,1,0:T(8,128)S(1)} %get-tuple-element.83), channel_id=1, source_target_pairs={{0,0},{1,1},{2,16},{3,17},{4,32},{5,33},{6,48},{7,49},{8,8},{9,9},... | collective-permute-start | bytes 98312 | tf_op jit(solution)/shard_map/ppermute | solution.py:421
  255.7 5.3 %collective-permute-done.25 = f32[2,32,128]{2,1,0:T(8,128)S(1)} collective-permute-done((f32[2,32,128]{2,1,0:T(8,128)S(1)}, f32[2,32,128]{2,1,0:T(8,128)S(1)}, u32[]{:S(2)}, u32[]{:S(2)}) %collective-permute-start.25) | collective-permute-done | bytes 32800 | tf_op jit(solution)/shard_map/ppermute | solution.py:421
  267.7 5.8 %all-to-all-done.8 = f32[4,8,32,128]{3,2,1,0:T(8,128)S(1)} async-done(((f32[4,8,32,128]{3,2,1,0:T(8,128)}), f32[4,8,32,128]{3,2,1,0:T(8,128)S(1)}, u32[]{:S(2)}, u32[]{:S(2)}) %all-to-all-start.8) | async-done | bytes 524320 | tf_op jit(solution)/shard_map/all_to_all | solution.py:70
  (163 shorter events, 97.0 us)
Async XLA Ops:
  7.2 63.1 %all-gather.6.cloned.1.call-start = ((), (), s32[]{:S(2)}) async-start(), calls=%async_computation.9 | async-start | bytes 4456448 | tf_op jit(solution)/shard_map/all_gather | solution.py:311
  10.7 18.8 %collective-permute-start = (f32[384,128]{1,0:T(8,128)S(1)}, f32[384,128]{1,0:T(8,128)S(1)}, u32[]{:S(2)}, u32[]{:S(2)}) collective-permute-start(f32[384,128]{1,0:T(8,128)S(1)} %get-tuple-element.69), channel_id=1, source_target_pairs={{0,0},{1,8},{2,2},{3,10},{4,4},{5,12},{6,6},{7,14},{8,1},{9,9},{10... | collective-permute-start | bytes 589832 | tf_op jit(solution)/shard_map/ppermute | solution.py:307
  11.4 18.2 %collective-permute-start.1 = (f32[384,128]{1,0:T(8,128)S(1)}, f32[384,128]{1,0:T(8,128)S(1)}, u32[]{:S(2)}, u32[]{:S(2)}) collective-permute-start(f32[384,128]{1,0:T(8,128)S(1)} %get-tuple-element.70), channel_id=1, source_target_pairs={{0,1},{1,9},{2,3},{3,11},{4,5},{5,13},{6,7},{7,15},{8,0},{9,8},{10... | collective-permute-start | bytes 589832 | tf_op jit(solution)/shard_map/ppermute | solution.py:307
  22.3 11.1 %all-to-all-start.1 = ((f32[4,4,32,128]{3,2,1,0:T(8,128)}), f32[4,4,32,128]{3,2,1,0:T(8,128)S(1)}, u32[]{:S(2)}, u32[]{:S(2)}) async-start(f32[4,4,32,128]{3,2,1,0:T(8,128)} %copy.23), calls=%async_computation.1 | async-start | bytes 524288 | tf_op jit(solution)/shard_map/all_to_all | solution.py:322
  30.3 9.6 %collective-permute-start.2 = (f32[768,128]{1,0:T(8,128)S(1)}, f32[768,128]{1,0:T(8,128)S(1)}, u32[]{:S(2)}, u32[]{:S(2)}) collective-permute-start(f32[768,128]{1,0:T(8,128)S(1)} %get-tuple-element.59), channel_id=1, source_target_pairs={{0,0},{1,8},{2,2},{3,10},{4,4},{5,12},{6,6},{7,14},{8,1},{9,9},{10... | collective-permute-start | bytes 1179656 | tf_op jit(solution)/shard_map/ppermute | solution.py:307
  31.0 34.9 %collective-permute-start.3 = (f32[768,128]{1,0:T(8,128)S(1)}, f32[768,128]{1,0:T(8,128)S(1)}, u32[]{:S(2)}, u32[]{:S(2)}) collective-permute-start(f32[768,128]{1,0:T(8,128)S(1)} %get-tuple-element.60), channel_id=1, source_target_pairs={{0,1},{1,9},{2,3},{3,11},{4,5},{5,13},{6,7},{7,15},{8,0},{9,8},{10... | collective-permute-start | bytes 1179656 | tf_op jit(solution)/shard_map/ppermute | solution.py:307
  34.5 32.4 %all-to-all-start = ((f32[4,2,256,128]{3,2,1,0:T(8,128)}), f32[4,2,256,128]{3,2,1,0:T(8,128)}, u32[]{:S(2)}, u32[]{:S(2)}) async-start(f32[4,2,256,128]{3,2,1,0:T(8,128)} %broadcast_in_dim.12), calls=%async_computation | async-start | bytes 2097152 | tf_op jit(solution)/shard_map/all_to_all | solution.py:70
  39.2 84.6 %all-gather.8.cloned.1.call-start = ((), (), s32[]{:S(2)}) async-start(), calls=%async_computation.10 | async-start | bytes 3932160 | tf_op jit(solution)/shard_map/all_gather | solution.py:325
  70.3 143.1 %all-gather.10.cloned.1.call-start = ((), (), s32[]{:S(2)}) async-start(), calls=%async_computation.11 | async-start | bytes 13369344 | tf_op jit(solution)/shard_map/all_gather | solution.py:341
  77.1 10.0 %collective-permute-start.4 = (f32[512,128]{1,0:T(8,128)}, f32[512,128]{1,0:T(8,128)S(1)}, u32[]{:S(2)}, u32[]{:S(2)}) collective-permute-start(f32[512,128]{1,0:T(8,128)} %shard_map.137.refs_2_), channel_id=1, source_target_pairs={{0,2},{2,4},{4,6},{6,8},{8,10},{10,12},{12,14},{14,0},{1,3},{3,5},... | collective-permute-start | bytes 786440 | tf_op jit(solution)/shard_map/ppermute | solution.py:60
  119.3 13.2 %all-to-all-start.2 = ((f32[4,256,128]{2,1,0:T(8,128)}), f32[4,256,128]{2,1,0:T(8,128)}, u32[]{:S(2)}, u32[]{:S(2)}) async-start(f32[4,256,128]{2,1,0:T(8,128)} %bitcast.122), calls=%async_computation.2 | async-start | bytes 1048576 | tf_op jit(solution)/shard_map/all_to_all | solution.py:363
  137.7 17.2 %all-to-all-start.4 = ((f32[4,2,224,128]{3,2,1,0:T(8,128)}), f32[4,2,224,128]{3,2,1,0:T(8,128)S(1)}, u32[]{:S(2)}, u32[]{:S(2)}) async-start(f32[4,2,224,128]{3,2,1,0:T(8,128)} %copy.24), calls=%async_computation.4 | async-start | bytes 1835008 | tf_op jit(solution)/shard_map/all_to_all | solution.py:374
  142.0 9.5 %collective-permute-start.12 = (f32[256,128]{1,0:T(8,128)S(1)}, f32[256,128]{1,0:T(8,128)S(1)}, u32[]{:S(2)}, u32[]{:S(2)}) collective-permute-start(f32[256,128]{1,0:T(8,128)S(1)} %bitcast_subtract_fusion.refs_2_), channel_id=1, source_target_pairs={{0,2},{2,4},{4,6},{6,8},{8,10},{10,12},{12,14},{14,0},{1,3},{3,5},... | collective-permute-start | bytes 393224 | tf_op jit(solution)/shard_map/ppermute | solution.py:60
  151.5 9.4 %collective-permute-start.14 = (f32[256,128]{1,0:T(8,128)S(1)}, f32[256,128]{1,0:T(8,128)S(1)}, u32[]{:S(2)}, u32[]{:S(2)}) collective-permute-start(f32[256,128]{1,0:T(8,128)S(1)} %collective-permute-done.12.refs_3_), channel_id=1, source_target_pairs={{0,2},{2,4},{4,6},{6,8},{8,10},{10,12},{12,14},{14,0},{1,3},{3,5},... | collective-permute-start | bytes 393224 | tf_op jit(solution)/shard_map/ppermute | solution.py:60
  151.5 9.4 %collective-permute-start.15 = (f32[256,128]{1,0:T(8,128)S(1)}, f32[256,128]{1,0:T(8,128)S(1)}, u32[]{:S(2)}, u32[]{:S(2)}) collective-permute-start(f32[256,128]{1,0:T(8,128)S(1)} %collective-permute-done.13.refs_4_), channel_id=1, source_target_pairs={{0,14},{2,0},{4,2},{6,4},{8,6},{10,8},{12,10},{14,12},{1,15},{3,1}... | collective-permute-start | bytes 393224 | tf_op jit(solution)/shard_map/ppermute | solution.py:61
  154.9 31.6 %all-to-all-start.3 = ((f32[4,2,2,128,128]{4,3,2,1,0:T(8,128)}), f32[4,2,2,128,128]{4,3,2,1,0:T(8,128)}, u32[]{:S(2)}, u32[]{:S(2)}) async-start(f32[4,2,2,128,128]{4,3,2,1,0:T(8,128)} %bitcast.29), calls=%async_computation.3 | async-start | bytes 2097152 | tf_op jit(solution)/shard_map/all_to_all | solution.py:367
  170.6 11.3 %collective-permute-start.21 = (f32[224,128]{1,0:T(8,128)S(1)}, f32[224,128]{1,0:T(8,128)S(1)}, u32[]{:S(2)}, u32[]{:S(2)}) collective-permute-start(f32[224,128]{1,0:T(8,128)S(1)} %get-tuple-element.76), channel_id=1, source_target_pairs={{0,8},{1,0},{2,10},{3,2},{4,12},{5,4},{6,14},{7,6},{8,9},{9,1},{10... | collective-permute-start | bytes 344072 | tf_op jit(solution)/shard_map/ppermute | solution.py:381
  174.9 10.2 %collective-permute-start.18 = (f32[128,128]{1,0:T(8,128)S(1)}, f32[128,128]{1,0:T(8,128)S(1)}, u32[]{:S(2)}, u32[]{:S(2)}) collective-permute-start(f32[128,128]{1,0:T(8,128)S(1)} %slice.55), channel_id=1, source_target_pairs={{0,2},{2,4},{4,6},{6,8},{8,10},{10,12},{12,14},{14,0},{1,3},{3,5},... | collective-permute-start | bytes 196616 | tf_op jit(solution)/shard_map/ppermute | solution.py:60
  175.2 11.4 %collective-permute-start.19 = (f32[128,128]{1,0:T(8,128)S(1)}, f32[128,128]{1,0:T(8,128)S(1)}, u32[]{:S(2)}, u32[]{:S(2)}) collective-permute-start(f32[128,128]{1,0:T(8,128)S(1)} %slice.56), channel_id=1, source_target_pairs={{0,14},{2,0},{4,2},{6,4},{8,6},{10,8},{12,10},{14,12},{1,15},{3,1}... | collective-permute-start | bytes 196616 | tf_op jit(solution)/shard_map/ppermute | solution.py:61
  187.6 19.6 %all-to-all-start.5 = ((f32[4,2,224,128]{3,2,1,0:T(8,128)}), f32[4,2,224,128]{3,2,1,0:T(8,128)}, u32[]{:S(2)}, u32[]{:S(2)}) async-start(f32[4,2,224,128]{3,2,1,0:T(8,128)} %broadcast_in_dim.13), calls=%async_computation.5 | async-start | bytes 1835008 | tf_op jit(solution)/shard_map/all_to_all | solution.py:70
  207.2 16.5 %all-to-all-start.6 = ((f32[4,2,64,128]{3,2,1,0:T(8,128)}), f32[4,2,64,128]{3,2,1,0:T(8,128)}, u32[]{:S(2)}, u32[]{:S(2)}) async-start(f32[4,2,64,128]{3,2,1,0:T(8,128)} %copy.26), calls=%async_computation.6 | async-start | bytes 524288 | tf_op jit(solution)/shard_map/all_to_all | solution.py:374
  223.7 22.1 %all-to-all-start.7 = ((f32[16,2,2,32,128]{4,3,2,1,0:T(8,128)}), f32[16,2,2,32,128]{4,3,2,1,0:T(8,128)S(1)}, u32[]{:S(2)}, u32[]{:S(2)}) async-start(f32[16,2,2,32,128]{4,3,2,1,0:T(8,128)} %bitcast.107), calls=%async_computation.7 | async-start | bytes 2097152 | tf_op jit(solution)/shard_map/all_to_all | solution.py:416
  245.9 9.8 %collective-permute-start.24 = (f32[2,32,128]{2,1,0:T(8,128)S(1)}, f32[2,32,128]{2,1,0:T(8,128)S(1)}, u32[]{:S(2)}, u32[]{:S(2)}) collective-permute-start(f32[2,32,128]{2,1,0:T(8,128)S(1)} %get-tuple-element.83), channel_id=1, source_target_pairs={{0,0},{1,1},{2,16},{3,17},{4,32},{5,33},{6,48},{7,49},{8,8},{9,9},... | collective-permute-start | bytes 98312 | tf_op jit(solution)/shard_map/ppermute | solution.py:421
  262.0 11.5 %all-to-all-start.8 = ((f32[4,8,32,128]{3,2,1,0:T(8,128)}), f32[4,8,32,128]{3,2,1,0:T(8,128)S(1)}, u32[]{:S(2)}, u32[]{:S(2)}) async-start(f32[4,8,32,128]{3,2,1,0:T(8,128)} %broadcast_in_dim.14), calls=%async_computation.8 | async-start | bytes 1048576 | tf_op jit(solution)/shard_map/all_to_all | solution.py:70
  (36 other events, 412.3 us)
Sparse Core Ops, SparseCore 0:
  9.8 60.4 all-gather.5
  72.1 37.5 all-gather.7
  111.9 92.1 all-gather.9

commit v3 on v2

--- a/solution.py
+++ b/solution.py
@@ -407,8 +407,9 @@
         *diag_pieces,
         terms=256 * 1024 * 256,
     )
+    late = summed([leaf_parent[0], leaf_parent[1]])
+    early, late = lax.optimization_barrier((early, late))
     early = everywhere(early)
-    late = summed([leaf_parent[0], leaf_parent[1]])
 
     cross = leaf_cross(core.reshape(1), pole_weights, leaf_parent, leaf_root, panels)
     cross, early = lax.optimization_barrier((cross, early))

time: 283 us -> 294 us (1.039)
  blocking collectives: 0 us -> 29.1 us
  starting transfers between devices: 101 us -> 89.4 us
  waiting for transfers between devices: 96.7 us -> 89.1 us
    all_to_all x0 -> x2, blocking collectives: none -> 29.1 us  [the longest x1 16.8 us: spread(): lax.all_to_all(jnp.broadcast_to(value[None], (size,) + value.shape), axis...]
    all_to_all x3 -> x2, waiting for transfers between devices: 13 us -> 5.83 us  [spread(): lax.all_to_all(jnp.broadcast_to(value[None], (size,) + value.shape), axis...]
    all_to_all x3 -> x2, starting transfers between devices: 13.1 us -> 8.15 us  [spread(): lax.all_to_all(jnp.broadcast_to(value[None], (size,) + value.shape), axis...]
    all_to_all x2 -> x1, starting transfers between devices: 8.29 us -> 4.24 us  [summed(): lax.all_to_all(jnp.moveaxis(blocks, 1, 0), 'pole', 0, 0)]
  transfers between devices with their start and end apart: 38 -> 36, of which waited for: 20 -> 19; matrix products, arithmetic and copies ran while one was open for 9% -> 9% of each run, Pallas kernels for 13% -> 9%
where the time goes in v3:
time: 294 us; the launch traced here: 292 us
  starting transfers between devices  89.4 us (30%)
  waiting for transfers between devices  89.1 us (30%)
  Pallas kernels  38 us (13%)
  blocking collectives  29.1 us (10%)
  local copies, waits for them, and re-layouts  15.9 us (5%)
  other arithmetic  15.6 us (5%)
  between operations  15.3 us (5%)
    ppermute x8, waiting for transfers between devices, onward(): lax.ppermute(ahead, RING, ring_pairs(1))  32.2 us
    pallas_call x4, Pallas kernels, with_copies(): pl.pallas_call(kernel, out_shape=[jax.ShapeDtypeStruct(shape, jnp.float32...  27.7 us
    ppermute x4, waiting for transfers between devices, to_ring(): lax.ppermute(piece, LANE, lane_pairs(lambda h, l, c: (c, l, h ^ flip)))  26 us
    ppermute x8, starting transfers between devices, onward(): lax.ppermute(behind, RING, ring_pairs(-1))  24.9 us
    all_to_all x1, blocking collectives, spread(): lax.all_to_all(jnp.broadcast_to(value[None], (size,) + value.shape), axis...  16.8 us
    all_to_all x1, blocking collectives, summed(): lax.all_to_all(jnp.moveaxis(blocks, 1, 0), 'pole', 0, 0)  12.4 us
    ppermute x4, starting transfers between devices, to_ring(): lax.ppermute(piece, LANE, lane_pairs(lambda h, l, c: (c, l, h ^ flip)))  11.3 us
    ppermute x4, starting transfers between devices, in_place(): lax.ppermute(piece, LANE, lane_pairs(lambda h, l, c: (c ^ flip, l, h)))  11.3 us
  transfers between devices with their start and end apart: 36, of which 19 were waited for; matrix products, arithmetic and copies ran while one was open for 9% of the time, Pallas kernels for 9%

profile of v3, /device:TPU:24, one launch (start us, length us, event | category | flops | bytes accessed | tf_op | source)
XLA Modules:
  0.0 292.4 jit_solution(8621447220583120755)
XLA Ops:
  11.4 8.6 %collective-permute-start.1 = (f32[384,128]{1,0:T(8,128)S(1)}, f32[384,128]{1,0:T(8,128)S(1)}, u32[]{:S(2)}, u32[]{:S(2)}) collective-permute-start(f32[384,128]{1,0:T(8,128)S(1)} %get-tuple-element.74), channel_id=1, source_target_pairs={{0,1},{1,9},{2,3},{3,11},{4,5},{5,13},{6,7},{7,15},{8,0},{9,8},{10... | collective-permute-start | bytes 589832 | tf_op jit(solution)/shard_map/ppermute | solution.py:307
  22.3 4.3 %all-to-all-start.1 = ((f32[4,4,32,128]{3,2,1,0:T(8,128)}), f32[4,4,32,128]{3,2,1,0:T(8,128)S(1)}, u32[]{:S(2)}, u32[]{:S(2)}) async-start(f32[4,4,32,128]{3,2,1,0:T(8,128)} %copy.23), calls=%async_computation.1 | async-start | bytes 524288 | tf_op jit(solution)/shard_map/all_to_all | solution.py:322
  34.5 4.7 %all-to-all-start = ((f32[4,2,256,128]{3,2,1,0:T(8,128)}), f32[4,2,256,128]{3,2,1,0:T(8,128)}, u32[]{:S(2)}, u32[]{:S(2)}) async-start(f32[4,2,256,128]{3,2,1,0:T(8,128)} %broadcast_in_dim.12), calls=%async_computation | async-start | bytes 2097152 | tf_op jit(solution)/shard_map/all_to_all | solution.py:70
  39.9 26.0 %collective-permute-done.3 = f32[768,128]{1,0:T(8,128)S(1)} collective-permute-done((f32[768,128]{1,0:T(8,128)S(1)}, f32[768,128]{1,0:T(8,128)S(1)}, u32[]{:S(2)}, u32[]{:S(2)}) %collective-permute-start.3) | collective-permute-done | bytes 393248 | tf_op jit(solution)/shard_map/ppermute | solution.py:307
  70.4 6.8 %shard_map.137.refs_2_ = f32[512,128]{1,0:T(8,128)} custom-call(f32[16,256,256]{2,1,0:T(8,128)} %all-gather.6.cloned.1.call-done.inverse.refs_1_, f32[8,256,128]{2,1,0:T(8,128)} %bitcast.18.top), custom_call_target="tpu_custom_call" | custom-call | flops 805306368 | bytes 5505024 | tf_op jit(solution)/shard_map/pallas_call | solution.py:267
  80.4 6.6 %collective-permute-done.4.refs_3_ = f32[512,128]{1,0:T(8,128)S(1)} collective-permute-done((f32[512,128]{1,0:T(8,128)}, f32[512,128]{1,0:T(8,128)S(1)}, u32[]{:S(2)}, u32[]{:S(2)}) %collective-permute-start.4) | collective-permute-done | bytes 262176 | tf_op jit(solution)/shard_map/ppermute | solution.py:60
  90.3 5.7 %collective-permute-done.6.refs_5_ = f32[512,128]{1,0:T(8,128)S(1)} collective-permute-done((f32[512,128]{1,0:T(8,128)S(1)}, f32[512,128]{1,0:T(8,128)S(1)}, u32[]{:S(2)}, u32[]{:S(2)}) %collective-permute-start.6) | collective-permute-done | bytes 262176 | tf_op jit(solution)/shard_map/ppermute | solution.py:60
  99.4 4.8 %collective-permute-done.8.refs_7_ = f32[512,128]{1,0:T(8,128)S(1)} collective-permute-done((f32[512,128]{1,0:T(8,128)S(1)}, f32[512,128]{1,0:T(8,128)S(1)}, u32[]{:S(2)}, u32[]{:S(2)}) %collective-permute-start.8) | collective-permute-done | bytes 262176 | tf_op jit(solution)/shard_map/ppermute | solution.py:60
  112.8 6.5 %shard_map.138 = (f32[8,128,128]{2,1,0:T(8,128)}, f32[8,2,128,128]{3,2,1,0:T(8,128)}) custom-call(s32[8]{0:T(128)} %stack.71.order, f32[2,256,128]{2,1,0:T(8,128)} %copy-done.4, f32[2,768,128]{2,1,0:T(8,128)} %pad_maximum_fusion.refs_1_, f32[512,128]{1,0:T(8,128)} %shard_map.137.refs_2_, f32[512,128]{1,0:T(8,128)} %copy-done.10, f32[512,128]{1,0:T(8,128)} %copy-done.11, ...), custom_call_target="tpu_custom_call" | custom-call | flops 1207959552 | bytes 4718592 | tf_op jit(solution)/shard_map/pallas_call | solution.py:267
  119.4 4.5 %all-to-all-start.2 = ((f32[4,256,128]{2,1,0:T(8,128)}), f32[4,256,128]{2,1,0:T(8,128)}, u32[]{:S(2)}, u32[]{:S(2)}) async-start(f32[4,256,128]{2,1,0:T(8,128)} %bitcast.122), calls=%async_computation.2 | async-start | bytes 1048576 | tf_op jit(solution)/shard_map/all_to_all | solution.py:363
  123.9 8.6 %shard_map.139.root = f32[2,512,128]{2,1,0:T(8,128)} custom-call(s32[8]{0:T(128)} %stack.71.order, f32[8,768,128]{2,1,0:T(8,128)} %all-gather.8.cloned.1.call-done.refs_0_, f32[16,256,256]{2,1,0:T(8,128)} %all-gather.6.cloned.1.call-done.inverse.refs_1_, f32[512,128]{1,0:T(8,128)} %shard_map.137.refs_2_, f32[512,128]{1,0:T(8,128)} %copy-done.10, ...), custom_call_target="tpu_custom_call" | custom-call | flops 2415919104 | bytes 9961472 | tf_op jit(solution)/shard_map/pallas_call | solution.py:267
  145.8 5.8 %collective-permute-done.12.refs_3_ = f32[256,128]{1,0:T(8,128)S(1)} collective-permute-done((f32[256,128]{1,0:T(8,128)S(1)}, f32[256,128]{1,0:T(8,128)S(1)}, u32[]{:S(2)}, u32[]{:S(2)}) %collective-permute-start.12) | collective-permute-done | bytes 131104 | tf_op jit(solution)/shard_map/ppermute | solution.py:60
  155.0 4.8 %all-to-all-start.3 = ((f32[4,2,2,128,128]{4,3,2,1,0:T(8,128)}), f32[4,2,2,128,128]{4,3,2,1,0:T(8,128)}, u32[]{:S(2)}, u32[]{:S(2)}) async-start(f32[4,2,2,128,128]{4,3,2,1,0:T(8,128)} %bitcast.29), calls=%async_computation.3 | async-start | bytes 2097152 | tf_op jit(solution)/shard_map/all_to_all | solution.py:367
  164.5 5.4 %collective-permute-done.16.refs_7_ = f32[256,128]{1,0:T(8,128)S(1)} collective-permute-done((f32[256,128]{1,0:T(8,128)S(1)}, f32[256,128]{1,0:T(8,128)S(1)}, u32[]{:S(2)}, u32[]{:S(2)}) %collective-permute-start.16) | collective-permute-done | bytes 131104 | tf_op jit(solution)/shard_map/ppermute | solution.py:60
  187.2 5.8 %shard_map.140.parent = f32[2,256,128]{2,1,0:T(8,128)} custom-call(s32[8]{0:T(128)} %stack.71.order, f32[8,768,128]{2,1,0:T(8,128)} %all-gather.8.cloned.1.call-done.refs_0_, f32[4,2,2,128,128]{4,3,2,1,0:T(8,128)} %all-to-all-done.3.refs_1_, f32[256,128]{1,0:T(8,128)} %copy-done.7, f32[256,128]{1,0:T(8,128)} %copy-done.15, f32[256,128]{1,0:T(8,128)} %copy-done.16, ...), custom_call_target="tpu_custom_call" | custom-call | flops 402653184 | bytes 5505024 | tf_op jit(solution)/shard_map/pallas_call | solution.py:267
  194.1 12.4 %all_to_all.45 = f32[4,2,64,128]{3,2,1,0:T(8,128)S(1)} all-to-all(f32[4,2,64,128]{3,2,1,0:T(8,128)S(1)} %copy.25), channel_id=1, replica_groups=mesh['pole'=4,'y'=4,'zh'=2,'zl'=4,'core'=2] {'pole'}, dimensions={0} | all-to-all | bytes 524288 | tf_op jit(solution)/shard_map/all_to_all | solution.py:374
  208.1 16.8 %all_to_all.46 = f32[4,2,224,128]{3,2,1,0:T(8,128)S(1)} all-to-all(f32[4,2,224,128]{3,2,1,0:T(8,128)S(1)} %broadcast_in_dim.13), channel_id=1, replica_groups=mesh['pole'=4,'y'=4,'zh'=2,'zl'=4,'core'=2] {'pole'}, dimensions={0} | all-to-all | bytes 1835008 | tf_op jit(solution)/shard_map/all_to_all | solution.py:70
  225.9 10.3 %shard_map.141 = f32[4,4,2,2,32,128]{5,4,3,2,1,0:T(8,128)} custom-call(s32[1]{0:T(128)} %bitcast.core, f32[1]{0:T(128)} %copy.37.weight, f32[2,256,128]{2,1,0:T(8,128)} %shard_map.140.parent, f32[2,512,128]{2,1,0:T(8,128)} %shard_map.139.root, f32[16,4,384,128]{3,2,1,0:T(8,128)} %bitcast.105), custom_call_target="tpu_custom_call" | custom-call | flops 1207959552 | bytes 8126464 | tf_op jit(solution)/shard_map/pallas_call | solution.py:229
  236.2 5.6 %all-to-all-start.7 = ((f32[16,2,2,32,128]{4,3,2,1,0:T(8,128)}), f32[16,2,2,32,128]{4,3,2,1,0:T(8,128)S(1)}, u32[]{:S(2)}, u32[]{:S(2)}) async-start(f32[16,2,2,32,128]{4,3,2,1,0:T(8,128)} %bitcast.107), calls=%async_computation.7 | async-start | bytes 2097152 | tf_op jit(solution)/shard_map/all_to_all | solution.py:417
  243.3 5.7 %collective-permute-start.23 = (f32[64,128]{1,0:T(8,128)S(1)}, f32[64,128]{1,0:T(8,128)S(1)}, u32[]{:S(2)}, u32[]{:S(2)}) collective-permute-start(f32[64,128]{1,0:T(8,128)S(1)} %get-tuple-element.84), channel_id=1, source_target_pairs={{0,8},{1,0},{2,10},{3,2},{4,12},{5,4},{6,14},{7,6},{8,9},{9,1},{10... | collective-permute-start | bytes 98312 | tf_op jit(solution)/shard_map/ppermute | solution.py:381
  250.6 5.4 %all-to-all-done.7 = f32[16,2,2,32,128]{4,3,2,1,0:T(8,128)S(1)} async-done(((f32[16,2,2,32,128]{4,3,2,1,0:T(8,128)}), f32[16,2,2,32,128]{4,3,2,1,0:T(8,128)S(1)}, u32[]{:S(2)}, u32[]{:S(2)}) %all-to-all-start.7) | async-done | bytes 1048608 | tf_op jit(solution)/shard_map/all_to_all | solution.py:417
  256.1 7.7 %collective-permute-start.24 = (f32[2,32,128]{2,1,0:T(8,128)S(1)}, f32[2,32,128]{2,1,0:T(8,128)S(1)}, u32[]{:S(2)}, u32[]{:S(2)}) collective-permute-start(f32[2,32,128]{2,1,0:T(8,128)S(1)} %get-tuple-element.87), channel_id=1, source_target_pairs={{0,0},{1,1},{2,16},{3,17},{4,32},{5,33},{6,48},{7,49},{8,8},{9,9},... | collective-permute-start | bytes 98312 | tf_op jit(solution)/shard_map/ppermute | solution.py:422
  265.9 5.2 %collective-permute-done.25 = f32[2,32,128]{2,1,0:T(8,128)S(1)} collective-permute-done((f32[2,32,128]{2,1,0:T(8,128)S(1)}, f32[2,32,128]{2,1,0:T(8,128)S(1)}, u32[]{:S(2)}, u32[]{:S(2)}) %collective-permute-start.25) | collective-permute-done | bytes 32800 | tf_op jit(solution)/shard_map/ppermute | solution.py:422
  278.5 5.8 %all-to-all-done.8 = f32[4,8,32,128]{3,2,1,0:T(8,128)S(1)} async-done(((f32[4,8,32,128]{3,2,1,0:T(8,128)}), f32[4,8,32,128]{3,2,1,0:T(8,128)S(1)}, u32[]{:S(2)}, u32[]{:S(2)}) %all-to-all-start.8) | async-done | bytes 524320 | tf_op jit(solution)/shard_map/all_to_all | solution.py:70
  (159 shorter events, 93.2 us)
Async XLA Ops:
  7.2 63.1 %all-gather.6.cloned.1.call-start = ((), (), s32[]{:S(2)}) async-start(), calls=%async_computation.9 | async-start | bytes 4456448 | tf_op jit(solution)/shard_map/all_gather | solution.py:311
  10.7 18.8 %collective-permute-start = (f32[384,128]{1,0:T(8,128)S(1)}, f32[384,128]{1,0:T(8,128)S(1)}, u32[]{:S(2)}, u32[]{:S(2)}) collective-permute-start(f32[384,128]{1,0:T(8,128)S(1)} %get-tuple-element.73), channel_id=1, source_target_pairs={{0,0},{1,8},{2,2},{3,10},{4,4},{5,12},{6,6},{7,14},{8,1},{9,9},{10... | collective-permute-start | bytes 589832 | tf_op jit(solution)/shard_map/ppermute | solution.py:307
  11.4 18.2 %collective-permute-start.1 = (f32[384,128]{1,0:T(8,128)S(1)}, f32[384,128]{1,0:T(8,128)S(1)}, u32[]{:S(2)}, u32[]{:S(2)}) collective-permute-start(f32[384,128]{1,0:T(8,128)S(1)} %get-tuple-element.74), channel_id=1, source_target_pairs={{0,1},{1,9},{2,3},{3,11},{4,5},{5,13},{6,7},{7,15},{8,0},{9,8},{10... | collective-permute-start | bytes 589832 | tf_op jit(solution)/shard_map/ppermute | solution.py:307
  22.3 11.1 %all-to-all-start.1 = ((f32[4,4,32,128]{3,2,1,0:T(8,128)}), f32[4,4,32,128]{3,2,1,0:T(8,128)S(1)}, u32[]{:S(2)}, u32[]{:S(2)}) async-start(f32[4,4,32,128]{3,2,1,0:T(8,128)} %copy.23), calls=%async_computation.1 | async-start | bytes 524288 | tf_op jit(solution)/shard_map/all_to_all | solution.py:322
  30.3 9.6 %collective-permute-start.2 = (f32[768,128]{1,0:T(8,128)S(1)}, f32[768,128]{1,0:T(8,128)S(1)}, u32[]{:S(2)}, u32[]{:S(2)}) collective-permute-start(f32[768,128]{1,0:T(8,128)S(1)} %get-tuple-element.63), channel_id=1, source_target_pairs={{0,0},{1,8},{2,2},{3,10},{4,4},{5,12},{6,6},{7,14},{8,1},{9,9},{10... | collective-permute-start | bytes 1179656 | tf_op jit(solution)/shard_map/ppermute | solution.py:307
  31.0 34.9 %collective-permute-start.3 = (f32[768,128]{1,0:T(8,128)S(1)}, f32[768,128]{1,0:T(8,128)S(1)}, u32[]{:S(2)}, u32[]{:S(2)}) collective-permute-start(f32[768,128]{1,0:T(8,128)S(1)} %get-tuple-element.64), channel_id=1, source_target_pairs={{0,1},{1,9},{2,3},{3,11},{4,5},{5,13},{6,7},{7,15},{8,0},{9,8},{10... | collective-permute-start | bytes 1179656 | tf_op jit(solution)/shard_map/ppermute | solution.py:307
  34.5 32.4 %all-to-all-start = ((f32[4,2,256,128]{3,2,1,0:T(8,128)}), f32[4,2,256,128]{3,2,1,0:T(8,128)}, u32[]{:S(2)}, u32[]{:S(2)}) async-start(f32[4,2,256,128]{3,2,1,0:T(8,128)} %broadcast_in_dim.12), calls=%async_computation | async-start | bytes 2097152 | tf_op jit(solution)/shard_map/all_to_all | solution.py:70
  39.2 84.7 %all-gather.8.cloned.1.call-start = ((), (), s32[]{:S(2)}) async-start(), calls=%async_computation.10 | async-start | bytes 3932160 | tf_op jit(solution)/shard_map/all_gather | solution.py:325
  70.3 155.6 %all-gather.10.cloned.1.call-start = ((), (), s32[]{:S(2)}) async-start(), calls=%async_computation.11 | async-start | bytes 13369344 | tf_op jit(solution)/shard_map/all_gather | solution.py:341
  77.1 10.0 %collective-permute-start.4 = (f32[512,128]{1,0:T(8,128)}, f32[512,128]{1,0:T(8,128)S(1)}, u32[]{:S(2)}, u32[]{:S(2)}) collective-permute-start(f32[512,128]{1,0:T(8,128)} %shard_map.137.refs_2_), channel_id=1, source_target_pairs={{0,2},{2,4},{4,6},{6,8},{8,10},{10,12},{12,14},{14,0},{1,3},{3,5},... | collective-permute-start | bytes 786440 | tf_op jit(solution)/shard_map/ppermute | solution.py:60
  96.1 9.1 %collective-permute-start.9 = (f32[512,128]{1,0:T(8,128)S(1)}, f32[512,128]{1,0:T(8,128)S(1)}, u32[]{:S(2)}, u32[]{:S(2)}) collective-permute-start(f32[512,128]{1,0:T(8,128)S(1)} %collective-permute-done.7.refs_6_), channel_id=1, source_target_pairs={{0,14},{2,0},{4,2},{6,4},{8,6},{10,8},{12,10},{14,12},{1,15},{3,1}... | collective-permute-start | bytes 786440 | tf_op jit(solution)/shard_map/ppermute | solution.py:61
  119.4 13.2 %all-to-all-start.2 = ((f32[4,256,128]{2,1,0:T(8,128)}), f32[4,256,128]{2,1,0:T(8,128)}, u32[]{:S(2)}, u32[]{:S(2)}) async-start(f32[4,256,128]{2,1,0:T(8,128)} %bitcast.122), calls=%async_computation.2 | async-start | bytes 1048576 | tf_op jit(solution)/shard_map/all_to_all | solution.py:363
  137.7 17.3 %all-to-all-start.4 = ((f32[4,2,224,128]{3,2,1,0:T(8,128)}), f32[4,2,224,128]{3,2,1,0:T(8,128)S(1)}, u32[]{:S(2)}, u32[]{:S(2)}) async-start(f32[4,2,224,128]{3,2,1,0:T(8,128)} %copy.24), calls=%async_computation.4 | async-start | bytes 1835008 | tf_op jit(solution)/shard_map/all_to_all | solution.py:374
  142.0 9.6 %collective-permute-start.12 = (f32[256,128]{1,0:T(8,128)S(1)}, f32[256,128]{1,0:T(8,128)S(1)}, u32[]{:S(2)}, u32[]{:S(2)}) collective-permute-start(f32[256,128]{1,0:T(8,128)S(1)} %bitcast_subtract_fusion.refs_2_), channel_id=1, source_target_pairs={{0,2},{2,4},{4,6},{6,8},{8,10},{10,12},{12,14},{14,0},{1,3},{3,5},... | collective-permute-start | bytes 393224 | tf_op jit(solution)/shard_map/ppermute | solution.py:60
  142.2 9.4 %collective-permute-start.13 = (f32[256,128]{1,0:T(8,128)S(1)}, f32[256,128]{1,0:T(8,128)S(1)}, u32[]{:S(2)}, u32[]{:S(2)}) collective-permute-start(f32[256,128]{1,0:T(8,128)S(1)} %bitcast_subtract_fusion.refs_2_), channel_id=1, source_target_pairs={{0,14},{2,0},{4,2},{6,4},{8,6},{10,8},{12,10},{14,12},{1,15},{3,1}... | collective-permute-start | bytes 393224 | tf_op jit(solution)/shard_map/ppermute | solution.py:61
  151.6 9.4 %collective-permute-start.14 = (f32[256,128]{1,0:T(8,128)S(1)}, f32[256,128]{1,0:T(8,128)S(1)}, u32[]{:S(2)}, u32[]{:S(2)}) collective-permute-start(f32[256,128]{1,0:T(8,128)S(1)} %collective-permute-done.12.refs_3_), channel_id=1, source_target_pairs={{0,2},{2,4},{4,6},{6,8},{8,10},{10,12},{12,14},{14,0},{1,3},{3,5},... | collective-permute-start | bytes 393224 | tf_op jit(solution)/shard_map/ppermute | solution.py:60
  151.6 9.4 %collective-permute-start.15 = (f32[256,128]{1,0:T(8,128)S(1)}, f32[256,128]{1,0:T(8,128)S(1)}, u32[]{:S(2)}, u32[]{:S(2)}) collective-permute-start(f32[256,128]{1,0:T(8,128)S(1)} %collective-permute-done.13.refs_4_), channel_id=1, source_target_pairs={{0,14},{2,0},{4,2},{6,4},{8,6},{10,8},{12,10},{14,12},{1,15},{3,1}... | collective-permute-start | bytes 393224 | tf_op jit(solution)/shard_map/ppermute | solution.py:61
  155.0 32.2 %all-to-all-start.3 = ((f32[4,2,2,128,128]{4,3,2,1,0:T(8,128)}), f32[4,2,2,128,128]{4,3,2,1,0:T(8,128)}, u32[]{:S(2)}, u32[]{:S(2)}) async-start(f32[4,2,2,128,128]{4,3,2,1,0:T(8,128)} %bitcast.29), calls=%async_computation.3 | async-start | bytes 2097152 | tf_op jit(solution)/shard_map/all_to_all | solution.py:367
  170.6 11.2 %collective-permute-start.21 = (f32[224,128]{1,0:T(8,128)S(1)}, f32[224,128]{1,0:T(8,128)S(1)}, u32[]{:S(2)}, u32[]{:S(2)}) collective-permute-start(f32[224,128]{1,0:T(8,128)S(1)} %get-tuple-element.80), channel_id=1, source_target_pairs={{0,8},{1,0},{2,10},{3,2},{4,12},{5,4},{6,14},{7,6},{8,9},{9,1},{10... | collective-permute-start | bytes 344072 | tf_op jit(solution)/shard_map/ppermute | solution.py:381
  174.9 10.2 %collective-permute-start.18 = (f32[128,128]{1,0:T(8,128)S(1)}, f32[128,128]{1,0:T(8,128)S(1)}, u32[]{:S(2)}, u32[]{:S(2)}) collective-permute-start(f32[128,128]{1,0:T(8,128)S(1)} %slice.55), channel_id=1, source_target_pairs={{0,2},{2,4},{4,6},{6,8},{8,10},{10,12},{12,14},{14,0},{1,3},{3,5},... | collective-permute-start | bytes 196616 | tf_op jit(solution)/shard_map/ppermute | solution.py:60
  175.2 11.4 %collective-permute-start.19 = (f32[128,128]{1,0:T(8,128)S(1)}, f32[128,128]{1,0:T(8,128)S(1)}, u32[]{:S(2)}, u32[]{:S(2)}) collective-permute-start(f32[128,128]{1,0:T(8,128)S(1)} %slice.56), channel_id=1, source_target_pairs={{0,14},{2,0},{4,2},{6,4},{8,6},{10,8},{12,10},{14,12},{1,15},{3,1}... | collective-permute-start | bytes 196616 | tf_op jit(solution)/shard_map/ppermute | solution.py:61
  236.2 19.8 %all-to-all-start.7 = ((f32[16,2,2,32,128]{4,3,2,1,0:T(8,128)}), f32[16,2,2,32,128]{4,3,2,1,0:T(8,128)S(1)}, u32[]{:S(2)}, u32[]{:S(2)}) async-start(f32[16,2,2,32,128]{4,3,2,1,0:T(8,128)} %bitcast.107), calls=%async_computation.7 | async-start | bytes 2097152 | tf_op jit(solution)/shard_map/all_to_all | solution.py:417
  256.1 9.8 %collective-permute-start.24 = (f32[2,32,128]{2,1,0:T(8,128)S(1)}, f32[2,32,128]{2,1,0:T(8,128)S(1)}, u32[]{:S(2)}, u32[]{:S(2)}) collective-permute-start(f32[2,32,128]{2,1,0:T(8,128)S(1)} %get-tuple-element.87), channel_id=1, source_target_pairs={{0,0},{1,1},{2,16},{3,17},{4,32},{5,33},{6,48},{7,49},{8,8},{9,9},... | collective-permute-start | bytes 98312 | tf_op jit(solution)/shard_map/ppermute | solution.py:422
  272.8 11.5 %all-to-all-start.8 = ((f32[4,8,32,128]{3,2,1,0:T(8,128)}), f32[4,8,32,128]{3,2,1,0:T(8,128)S(1)}, u32[]{:S(2)}, u32[]{:S(2)}) async-start(f32[4,8,32,128]{3,2,1,0:T(8,128)} %broadcast_in_dim.14), calls=%async_computation.8 | async-start | bytes 1048576 | tf_op jit(solution)/shard_map/all_to_all | solution.py:70
  (33 other events, 344.1 us)
Sparse Core Ops, SparseCore 0:
  9.8 60.4 all-gather.5
  72.1 37.5 all-gather.7
  111.9 92.1 all-gather.9

commit v4 on v2

--- a/solution.py
+++ b/solution.py
@@ -199,52 +199,58 @@
             out[leaf, rows, :] = -(total[rows, leaf * 128 : (leaf + 1) * 128] + added)
 
 
-def leaf_kernel(core, weight, parent, root, panels, out, total, high, low):
-    block, half = pl.program_id(0), pl.program_id(1)
-
-    @pl.when(block == 0)
+def leaf_kernel(core, weight, parent, root, panels, out, high, low):
+    @pl.when(pl.program_id(0) == 0)
     def _():
         for leaf in range(2):
-            rows = jnp.concatenate([parent[leaf], root[leaf]], axis=0)
-            high[half, leaf], low[half, leaf] = split(jnp.transpose(rows))
+            rows = jnp.concatenate(
+                [
+                    parent[leaf, 0:128, :],
+                    root[leaf, 0:256, :],
+                    parent[leaf, 128:256, :],
+                    root[leaf, 256:512, :],
+                ],
+                axis=0,
+            )
+            high[leaf], low[leaf] = split(jnp.transpose(rows))
 
     for leaf in range(2):
-        right = split(jnp.concatenate([panels[0, leaf], panels[1, leaf]], axis=1))
-        part = product((high[half, leaf], low[half, leaf]), right)
-
-        @pl.when(half == 0)
-        def _():
-            total[leaf] = part
-
-        @pl.when(half == 1)
-        def _():
-            done = weight[0] * (total[leaf] + part)
-            for side in range(2):
-                out[:, 0, side, leaf] = done[:, side * 128 : (side + 1) * 128].reshape(
-                    SIZE_X, 32, 128
-                )
+        right = jnp.concatenate(
+            [
+                jnp.concatenate([panels[half, 0, 0, leaf], panels[half, 0, 1, leaf]], axis=1)
+                for half in range(SIZE_H)
+            ],
+            axis=0,
+        )
+        done = weight[0] * product((high[leaf], low[leaf]), split(right))
+        for side in range(2):
+            out[:, 0, side, leaf] = done[:, side * 128 : (side + 1) * 128].reshape(
+                SIZE_X, 32, 128
+            )
 
 
 def leaf_cross(core, weight, parent, root, panels):
+    panels = panels.reshape(SIZE_H, SIZE_L, SIZE_C, 4, 384, 128)
     return pl.pallas_call(
         leaf_kernel,
         out_shape=jax.ShapeDtypeStruct((SIZE_X, SIZE_Y, 2, 2, 32, 128), jnp.float32),
         grid_spec=pltpu.PrefetchScalarGridSpec(
             num_scalar_prefetch=1,
-            grid=(SIZE_L, SIZE_H),
+            grid=(SIZE_L,),
             in_specs=[
                 IN_SMEM,
-                pl.BlockSpec((2, 128, 128), lambda l, h, core: (0, h, 0)),
-                pl.BlockSpec((2, 256, 128), lambda l, h, core: (0, h, 0)),
-                pl.BlockSpec((2, 2, 384, 128), lambda l, h, core: (h * 4 + l, core[0], 0, 0)),
+                pl.BlockSpec((2, 256, 128), lambda l, core: (0, 0, 0)),
+                pl.BlockSpec((2, 512, 128), lambda l, core: (0, 0, 0)),
+                pl.BlockSpec(
+                    (SIZE_H, 1, SIZE_C, 2, 384, 128), lambda l, core: (0, l, 0, core[0], 0, 0)
+                ),
             ],
             out_specs=pl.BlockSpec(
-                (SIZE_X, 1, 2, 2, 32, 128), lambda l, h, core: (0, l, 0, 0, 0, 0)
+                (SIZE_X, 1, 2, 2, 32, 128), lambda l, core: (0, l, 0, 0, 0, 0)
             ),
             scratch_shapes=[
-                pltpu.VMEM((2, 128, 256), jnp.float32),
-                pltpu.VMEM((2, 2, 128, 384), jnp.bfloat16),
-                pltpu.VMEM((2, 2, 128, 384), jnp.bfloat16),
+                pltpu.VMEM((2, 128, 768), jnp.bfloat16),
+                pltpu.VMEM((2, 128, 768), jnp.bfloat16),
             ],
         ),
         cost_estimate=cost(2 * 768 * 1024 * 128, [(2, 768, 1024), (2, 768, 128), (2, 1024, 128)]),

time: 283 us -> 278 us (0.982)
  Pallas kernels: 38 us -> 33.5 us
    pallas_call x1, Pallas kernels: 10.3 us -> 5.83 us  [leaf_cross(): pl.pallas_call(leaf_kernel, out_shape=jax.ShapeDtypeStruct((SIZE_X, SIZE_...]
  transfers between devices with their start and end apart: 38 -> 38, of which waited for: 20 -> 20; matrix products, arithmetic and copies ran while one was open for 9% -> 9% of each run, Pallas kernels for 13% -> 12%
where the time goes in v4:
time: 278 us; the launch traced here: 277 us
  starting transfers between devices  101 us (36%)
  waiting for transfers between devices  96.7 us (35%)
  Pallas kernels  33.5 us (12%)
  local copies, waits for them, and re-layouts  16.4 us (6%)
  between operations  15.3 us (6%)
  other arithmetic  14.4 us (5%)
    ppermute x8, waiting for transfers between devices, onward(): lax.ppermute(ahead, RING, ring_pairs(1))  32.9 us
    pallas_call x4, Pallas kernels, with_copies(): pl.pallas_call(kernel, out_shape=[jax.ShapeDtypeStruct(shape, jnp.float32...  27.7 us
    ppermute x4, waiting for transfers between devices, to_ring(): lax.ppermute(piece, LANE, lane_pairs(lambda h, l, c: (c, l, h ^ flip)))  26 us
    ppermute x8, starting transfers between devices, onward(): lax.ppermute(behind, RING, ring_pairs(-1))  25 us
    all_to_all x3, starting transfers between devices, spread(): lax.all_to_all(jnp.broadcast_to(value[None], (size,) + value.shape), axis...  13.1 us
    all_to_all x3, waiting for transfers between devices, spread(): lax.all_to_all(jnp.broadcast_to(value[None], (size,) + value.shape), axis...  13 us
    ppermute x4, starting transfers between devices, to_ring(): lax.ppermute(piece, LANE, lane_pairs(lambda h, l, c: (c, l, h ^ flip)))  11.3 us
    ppermute x4, starting transfers between devices, in_place(): lax.ppermute(piece, LANE, lane_pairs(lambda h, l, c: (c ^ flip, l, h)))  11.2 us
  transfers between devices with their start and end apart: 38, of which 20 were waited for; matrix products, arithmetic and copies ran while one was open for 9% of the time, Pallas kernels for 12%

profile of v4, /device:TPU:24, one launch (start us, length us, event | category | flops | bytes accessed | tf_op | source)
XLA Modules:
  0.0 277.1 jit_solution(3011800376896714848)
XLA Ops:
  11.4 8.6 %collective-permute-start.1 = (f32[384,128]{1,0:T(8,128)S(1)}, f32[384,128]{1,0:T(8,128)S(1)}, u32[]{:S(2)}, u32[]{:S(2)}) collective-permute-start(f32[384,128]{1,0:T(8,128)S(1)} %get-tuple-element.70), channel_id=1, source_target_pairs={{0,1},{1,9},{2,3},{3,11},{4,5},{5,13},{6,7},{7,15},{8,0},{9,8},{10... | collective-permute-start | bytes 589832 | tf_op jit(solution)/shard_map/ppermute | solution.py:313
  34.5 4.7 %all-to-all-start = ((f32[4,2,256,128]{3,2,1,0:T(8,128)}), f32[4,2,256,128]{3,2,1,0:T(8,128)}, u32[]{:S(2)}, u32[]{:S(2)}) async-start(f32[4,2,256,128]{3,2,1,0:T(8,128)} %broadcast_in_dim.12), calls=%async_computation | async-start | bytes 2097152 | tf_op jit(solution)/shard_map/all_to_all | solution.py:70
  39.9 26.0 %collective-permute-done.3 = f32[768,128]{1,0:T(8,128)S(1)} collective-permute-done((f32[768,128]{1,0:T(8,128)S(1)}, f32[768,128]{1,0:T(8,128)S(1)}, u32[]{:S(2)}, u32[]{:S(2)}) %collective-permute-start.3) | collective-permute-done | bytes 393248 | tf_op jit(solution)/shard_map/ppermute | solution.py:313
  70.4 6.8 %shard_map.137.refs_2_ = f32[512,128]{1,0:T(8,128)} custom-call(f32[16,256,256]{2,1,0:T(8,128)} %all-gather.6.cloned.1.call-done.inverse.refs_1_, f32[8,256,128]{2,1,0:T(8,128)} %bitcast.18.top), custom_call_target="tpu_custom_call" | custom-call | flops 805306368 | bytes 5505024 | tf_op jit(solution)/shard_map/pallas_call | solution.py:273
  80.4 6.6 %collective-permute-done.4.refs_3_ = f32[512,128]{1,0:T(8,128)S(1)} collective-permute-done((f32[512,128]{1,0:T(8,128)}, f32[512,128]{1,0:T(8,128)S(1)}, u32[]{:S(2)}, u32[]{:S(2)}) %collective-permute-start.4) | collective-permute-done | bytes 262176 | tf_op jit(solution)/shard_map/ppermute | solution.py:60
  90.3 5.7 %collective-permute-done.6.refs_5_ = f32[512,128]{1,0:T(8,128)S(1)} collective-permute-done((f32[512,128]{1,0:T(8,128)S(1)}, f32[512,128]{1,0:T(8,128)S(1)}, u32[]{:S(2)}, u32[]{:S(2)}) %collective-permute-start.6) | collective-permute-done | bytes 262176 | tf_op jit(solution)/shard_map/ppermute | solution.py:60
  99.4 4.8 %collective-permute-done.8.refs_7_ = f32[512,128]{1,0:T(8,128)S(1)} collective-permute-done((f32[512,128]{1,0:T(8,128)S(1)}, f32[512,128]{1,0:T(8,128)S(1)}, u32[]{:S(2)}, u32[]{:S(2)}) %collective-permute-start.8) | collective-permute-done | bytes 262176 | tf_op jit(solution)/shard_map/ppermute | solution.py:60
  112.8 6.5 %shard_map.138 = (f32[8,128,128]{2,1,0:T(8,128)}, f32[8,2,128,128]{3,2,1,0:T(8,128)}) custom-call(s32[8]{0:T(128)} %stack.71.order, f32[2,256,128]{2,1,0:T(8,128)} %copy-done.4, f32[2,768,128]{2,1,0:T(8,128)} %pad_maximum_fusion.refs_1_, f32[512,128]{1,0:T(8,128)} %shard_map.137.refs_2_, f32[512,128]{1,0:T(8,128)} %copy-done.10, f32[512,128]{1,0:T(8,128)} %copy-done.11, ...), custom_call_target="tpu_custom_call" | custom-call | flops 1207959552 | bytes 4718592 | tf_op jit(solution)/shard_map/pallas_call | solution.py:273
  119.3 4.5 %all-to-all-start.2 = ((f32[4,256,128]{2,1,0:T(8,128)}), f32[4,256,128]{2,1,0:T(8,128)}, u32[]{:S(2)}, u32[]{:S(2)}) async-start(f32[4,256,128]{2,1,0:T(8,128)} %bitcast.122), calls=%async_computation.2 | async-start | bytes 1048576 | tf_op jit(solution)/shard_map/all_to_all | solution.py:369
  123.8 8.7 %shard_map.139.root = f32[2,512,128]{2,1,0:T(8,128)} custom-call(s32[8]{0:T(128)} %stack.71.order, f32[8,768,128]{2,1,0:T(8,128)} %all-gather.8.cloned.1.call-done.refs_0_, f32[16,256,256]{2,1,0:T(8,128)} %all-gather.6.cloned.1.call-done.inverse.refs_1_, f32[512,128]{1,0:T(8,128)} %shard_map.137.refs_2_, f32[512,128]{1,0:T(8,128)} %copy-done.10, ...), custom_call_target="tpu_custom_call" | custom-call | flops 2415919104 | bytes 9961472 | tf_op jit(solution)/shard_map/pallas_call | solution.py:273
  145.7 5.8 %collective-permute-done.12.refs_3_ = f32[256,128]{1,0:T(8,128)S(1)} collective-permute-done((f32[256,128]{1,0:T(8,128)S(1)}, f32[256,128]{1,0:T(8,128)S(1)}, u32[]{:S(2)}, u32[]{:S(2)}) %collective-permute-start.12) | collective-permute-done | bytes 131104 | tf_op jit(solution)/shard_map/ppermute | solution.py:60
  154.9 4.9 %all-to-all-start.3 = ((f32[4,2,2,128,128]{4,3,2,1,0:T(8,128)}), f32[4,2,2,128,128]{4,3,2,1,0:T(8,128)}, u32[]{:S(2)}, u32[]{:S(2)}) async-start(f32[4,2,2,128,128]{4,3,2,1,0:T(8,128)} %bitcast.29), calls=%async_computation.3 | async-start | bytes 2097152 | tf_op jit(solution)/shard_map/all_to_all | solution.py:373
  164.5 5.4 %collective-permute-done.16.refs_7_ = f32[256,128]{1,0:T(8,128)S(1)} collective-permute-done((f32[256,128]{1,0:T(8,128)S(1)}, f32[256,128]{1,0:T(8,128)S(1)}, u32[]{:S(2)}, u32[]{:S(2)}) %collective-permute-start.16) | collective-permute-done | bytes 131104 | tf_op jit(solution)/shard_map/ppermute | solution.py:60
  170.6 4.3 %collective-permute-start.21 = (f32[224,128]{1,0:T(8,128)S(1)}, f32[224,128]{1,0:T(8,128)S(1)}, u32[]{:S(2)}, u32[]{:S(2)}) collective-permute-start(f32[224,128]{1,0:T(8,128)S(1)} %get-tuple-element.76), channel_id=1, source_target_pairs={{0,8},{1,0},{2,10},{3,2},{4,12},{5,4},{6,14},{7,6},{8,9},{9,1},{10... | collective-permute-start | bytes 344072 | tf_op jit(solution)/shard_map/ppermute | solution.py:387
  187.6 5.0 %all-to-all-start.5 = ((f32[4,2,224,128]{3,2,1,0:T(8,128)}), f32[4,2,224,128]{3,2,1,0:T(8,128)}, u32[]{:S(2)}, u32[]{:S(2)}) async-start(f32[4,2,224,128]{3,2,1,0:T(8,128)} %broadcast_in_dim.13), calls=%async_computation.5 | async-start | bytes 1835008 | tf_op jit(solution)/shard_map/all_to_all | solution.py:70
  192.6 5.7 %shard_map.140.parent = f32[2,256,128]{2,1,0:T(8,128)} custom-call(s32[8]{0:T(128)} %stack.71.order, f32[8,768,128]{2,1,0:T(8,128)} %all-gather.8.cloned.1.call-done.refs_0_, f32[4,2,2,128,128]{4,3,2,1,0:T(8,128)} %all-to-all-done.3.refs_1_, f32[256,128]{1,0:T(8,128)} %copy-done.7, f32[256,128]{1,0:T(8,128)} %copy-done.16, f32[256,128]{1,0:T(8,128)} %copy-done.17, ...), custom_call_target="tpu_custom_call" | custom-call | flops 402653184 | bytes 5505024 | tf_op jit(solution)/shard_map/pallas_call | solution.py:273
  200.0 7.1 %all-to-all-done.5 = f32[4,2,224,128]{3,2,1,0:T(8,128)} async-done(((f32[4,2,224,128]{3,2,1,0:T(8,128)}), f32[4,2,224,128]{3,2,1,0:T(8,128)}, u32[]{:S(2)}, u32[]{:S(2)}) %all-to-all-start.5) | async-done | bytes 917536 | tf_op jit(solution)/shard_map/all_to_all | solution.py:70
  213.4 5.8 %shard_map.141 = f32[4,4,2,2,32,128]{5,4,3,2,1,0:T(8,128)} custom-call(s32[1]{0:T(128)} %bitcast.core, f32[1]{0:T(128)} %copy.37.weight, f32[2,256,128]{2,1,0:T(8,128)} %shard_map.140.parent, f32[2,512,128]{2,1,0:T(8,128)} %shard_map.139.root, f32[2,4,2,4,384,128]{5,4,3,2,1,0:T(8,128)} %bitcast.105), custom_call_target="tpu_custom_call" | custom-call | flops 1207959552 | bytes 8126464 | tf_op jit(solution)/shard_map/pallas_call | solution.py:234
  219.3 8.0 %all-to-all-start.7 = ((f32[16,2,2,32,128]{4,3,2,1,0:T(8,128)}), f32[16,2,2,32,128]{4,3,2,1,0:T(8,128)S(1)}, u32[]{:S(2)}, u32[]{:S(2)}) async-start(f32[16,2,2,32,128]{4,3,2,1,0:T(8,128)} %bitcast.107), calls=%async_computation.7 | async-start | bytes 2097152 | tf_op jit(solution)/shard_map/all_to_all | solution.py:422
  228.9 5.5 %collective-permute-start.23 = (f32[64,128]{1,0:T(8,128)S(1)}, f32[64,128]{1,0:T(8,128)S(1)}, u32[]{:S(2)}, u32[]{:S(2)}) collective-permute-start(f32[64,128]{1,0:T(8,128)S(1)} %get-tuple-element.80), channel_id=1, source_target_pairs={{0,8},{1,0},{2,10},{3,2},{4,12},{5,4},{6,14},{7,6},{8,9},{9,1},{10... | collective-permute-start | bytes 98312 | tf_op jit(solution)/shard_map/ppermute | solution.py:387
  236.1 5.3 %all-to-all-done.7 = f32[16,2,2,32,128]{4,3,2,1,0:T(8,128)S(1)} async-done(((f32[16,2,2,32,128]{4,3,2,1,0:T(8,128)}), f32[16,2,2,32,128]{4,3,2,1,0:T(8,128)S(1)}, u32[]{:S(2)}, u32[]{:S(2)}) %all-to-all-start.7) | async-done | bytes 1048608 | tf_op jit(solution)/shard_map/all_to_all | solution.py:422
  241.5 7.8 %collective-permute-start.24 = (f32[2,32,128]{2,1,0:T(8,128)S(1)}, f32[2,32,128]{2,1,0:T(8,128)S(1)}, u32[]{:S(2)}, u32[]{:S(2)}) collective-permute-start(f32[2,32,128]{2,1,0:T(8,128)S(1)} %get-tuple-element.83), channel_id=1, source_target_pairs={{0,0},{1,1},{2,16},{3,17},{4,32},{5,33},{6,48},{7,49},{8,8},{9,9},... | collective-permute-start | bytes 98312 | tf_op jit(solution)/shard_map/ppermute | solution.py:427
  251.3 5.3 %collective-permute-done.25 = f32[2,32,128]{2,1,0:T(8,128)S(1)} collective-permute-done((f32[2,32,128]{2,1,0:T(8,128)S(1)}, f32[2,32,128]{2,1,0:T(8,128)S(1)}, u32[]{:S(2)}, u32[]{:S(2)}) %collective-permute-start.25) | collective-permute-done | bytes 32800 | tf_op jit(solution)/shard_map/ppermute | solution.py:427
  263.2 5.8 %all-to-all-done.8 = f32[4,8,32,128]{3,2,1,0:T(8,128)S(1)} async-done(((f32[4,8,32,128]{3,2,1,0:T(8,128)}), f32[4,8,32,128]{3,2,1,0:T(8,128)S(1)}, u32[]{:S(2)}, u32[]{:S(2)}) %all-to-all-start.8) | async-done | bytes 524320 | tf_op jit(solution)/shard_map/all_to_all | solution.py:70
  (163 shorter events, 97.0 us)
Async XLA Ops:
  7.2 63.1 %all-gather.6.cloned.1.call-start = ((), (), s32[]{:S(2)}) async-start(), calls=%async_computation.9 | async-start | bytes 4456448 | tf_op jit(solution)/shard_map/all_gather | solution.py:317
  10.7 18.8 %collective-permute-start = (f32[384,128]{1,0:T(8,128)S(1)}, f32[384,128]{1,0:T(8,128)S(1)}, u32[]{:S(2)}, u32[]{:S(2)}) collective-permute-start(f32[384,128]{1,0:T(8,128)S(1)} %get-tuple-element.69), channel_id=1, source_target_pairs={{0,0},{1,8},{2,2},{3,10},{4,4},{5,12},{6,6},{7,14},{8,1},{9,9},{10... | collective-permute-start | bytes 589832 | tf_op jit(solution)/shard_map/ppermute | solution.py:313
  11.4 18.2 %collective-permute-start.1 = (f32[384,128]{1,0:T(8,128)S(1)}, f32[384,128]{1,0:T(8,128)S(1)}, u32[]{:S(2)}, u32[]{:S(2)}) collective-permute-start(f32[384,128]{1,0:T(8,128)S(1)} %get-tuple-element.70), channel_id=1, source_target_pairs={{0,1},{1,9},{2,3},{3,11},{4,5},{5,13},{6,7},{7,15},{8,0},{9,8},{10... | collective-permute-start | bytes 589832 | tf_op jit(solution)/shard_map/ppermute | solution.py:313
  22.3 11.1 %all-to-all-start.1 = ((f32[4,4,32,128]{3,2,1,0:T(8,128)}), f32[4,4,32,128]{3,2,1,0:T(8,128)S(1)}, u32[]{:S(2)}, u32[]{:S(2)}) async-start(f32[4,4,32,128]{3,2,1,0:T(8,128)} %copy.23), calls=%async_computation.1 | async-start | bytes 524288 | tf_op jit(solution)/shard_map/all_to_all | solution.py:328
  30.3 9.6 %collective-permute-start.2 = (f32[768,128]{1,0:T(8,128)S(1)}, f32[768,128]{1,0:T(8,128)S(1)}, u32[]{:S(2)}, u32[]{:S(2)}) collective-permute-start(f32[768,128]{1,0:T(8,128)S(1)} %get-tuple-element.59), channel_id=1, source_target_pairs={{0,0},{1,8},{2,2},{3,10},{4,4},{5,12},{6,6},{7,14},{8,1},{9,9},{10... | collective-permute-start | bytes 1179656 | tf_op jit(solution)/shard_map/ppermute | solution.py:313
  31.0 34.9 %collective-permute-start.3 = (f32[768,128]{1,0:T(8,128)S(1)}, f32[768,128]{1,0:T(8,128)S(1)}, u32[]{:S(2)}, u32[]{:S(2)}) collective-permute-start(f32[768,128]{1,0:T(8,128)S(1)} %get-tuple-element.60), channel_id=1, source_target_pairs={{0,1},{1,9},{2,3},{3,11},{4,5},{5,13},{6,7},{7,15},{8,0},{9,8},{10... | collective-permute-start | bytes 1179656 | tf_op jit(solution)/shard_map/ppermute | solution.py:313
  34.5 32.4 %all-to-all-start = ((f32[4,2,256,128]{3,2,1,0:T(8,128)}), f32[4,2,256,128]{3,2,1,0:T(8,128)}, u32[]{:S(2)}, u32[]{:S(2)}) async-start(f32[4,2,256,128]{3,2,1,0:T(8,128)} %broadcast_in_dim.12), calls=%async_computation | async-start | bytes 2097152 | tf_op jit(solution)/shard_map/all_to_all | solution.py:70
  39.2 84.6 %all-gather.8.cloned.1.call-start = ((), (), s32[]{:S(2)}) async-start(), calls=%async_computation.10 | async-start | bytes 3932160 | tf_op jit(solution)/shard_map/all_gather | solution.py:331
  70.3 143.1 %all-gather.10.cloned.1.call-start = ((), (), s32[]{:S(2)}) async-start(), calls=%async_computation.11 | async-start | bytes 13369344 | tf_op jit(solution)/shard_map/all_gather | solution.py:347
  77.1 10.0 %collective-permute-start.4 = (f32[512,128]{1,0:T(8,128)}, f32[512,128]{1,0:T(8,128)S(1)}, u32[]{:S(2)}, u32[]{:S(2)}) collective-permute-start(f32[512,128]{1,0:T(8,128)} %shard_map.137.refs_2_), channel_id=1, source_target_pairs={{0,2},{2,4},{4,6},{6,8},{8,10},{10,12},{12,14},{14,0},{1,3},{3,5},... | collective-permute-start | bytes 786440 | tf_op jit(solution)/shard_map/ppermute | solution.py:60
  119.3 13.2 %all-to-all-start.2 = ((f32[4,256,128]{2,1,0:T(8,128)}), f32[4,256,128]{2,1,0:T(8,128)}, u32[]{:S(2)}, u32[]{:S(2)}) async-start(f32[4,256,128]{2,1,0:T(8,128)} %bitcast.122), calls=%async_computation.2 | async-start | bytes 1048576 | tf_op jit(solution)/shard_map/all_to_all | solution.py:369
  137.7 17.2 %all-to-all-start.4 = ((f32[4,2,224,128]{3,2,1,0:T(8,128)}), f32[4,2,224,128]{3,2,1,0:T(8,128)S(1)}, u32[]{:S(2)}, u32[]{:S(2)}) async-start(f32[4,2,224,128]{3,2,1,0:T(8,128)} %copy.24), calls=%async_computation.4 | async-start | bytes 1835008 | tf_op jit(solution)/shard_map/all_to_all | solution.py:380
  142.0 9.5 %collective-permute-start.12 = (f32[256,128]{1,0:T(8,128)S(1)}, f32[256,128]{1,0:T(8,128)S(1)}, u32[]{:S(2)}, u32[]{:S(2)}) collective-permute-start(f32[256,128]{1,0:T(8,128)S(1)} %bitcast_subtract_fusion.refs_2_), channel_id=1, source_target_pairs={{0,2},{2,4},{4,6},{6,8},{8,10},{10,12},{12,14},{14,0},{1,3},{3,5},... | collective-permute-start | bytes 393224 | tf_op jit(solution)/shard_map/ppermute | solution.py:60
  151.5 9.4 %collective-permute-start.14 = (f32[256,128]{1,0:T(8,128)S(1)}, f32[256,128]{1,0:T(8,128)S(1)}, u32[]{:S(2)}, u32[]{:S(2)}) collective-permute-start(f32[256,128]{1,0:T(8,128)S(1)} %collective-permute-done.12.refs_3_), channel_id=1, source_target_pairs={{0,2},{2,4},{4,6},{6,8},{8,10},{10,12},{12,14},{14,0},{1,3},{3,5},... | collective-permute-start | bytes 393224 | tf_op jit(solution)/shard_map/ppermute | solution.py:60
  151.5 9.4 %collective-permute-start.15 = (f32[256,128]{1,0:T(8,128)S(1)}, f32[256,128]{1,0:T(8,128)S(1)}, u32[]{:S(2)}, u32[]{:S(2)}) collective-permute-start(f32[256,128]{1,0:T(8,128)S(1)} %collective-permute-done.13.refs_4_), channel_id=1, source_target_pairs={{0,14},{2,0},{4,2},{6,4},{8,6},{10,8},{12,10},{14,12},{1,15},{3,1}... | collective-permute-start | bytes 393224 | tf_op jit(solution)/shard_map/ppermute | solution.py:61
  154.9 31.6 %all-to-all-start.3 = ((f32[4,2,2,128,128]{4,3,2,1,0:T(8,128)}), f32[4,2,2,128,128]{4,3,2,1,0:T(8,128)}, u32[]{:S(2)}, u32[]{:S(2)}) async-start(f32[4,2,2,128,128]{4,3,2,1,0:T(8,128)} %bitcast.29), calls=%async_computation.3 | async-start | bytes 2097152 | tf_op jit(solution)/shard_map/all_to_all | solution.py:373
  170.6 11.3 %collective-permute-start.21 = (f32[224,128]{1,0:T(8,128)S(1)}, f32[224,128]{1,0:T(8,128)S(1)}, u32[]{:S(2)}, u32[]{:S(2)}) collective-permute-start(f32[224,128]{1,0:T(8,128)S(1)} %get-tuple-element.76), channel_id=1, source_target_pairs={{0,8},{1,0},{2,10},{3,2},{4,12},{5,4},{6,14},{7,6},{8,9},{9,1},{10... | collective-permute-start | bytes 344072 | tf_op jit(solution)/shard_map/ppermute | solution.py:387
  174.9 10.2 %collective-permute-start.18 = (f32[128,128]{1,0:T(8,128)S(1)}, f32[128,128]{1,0:T(8,128)S(1)}, u32[]{:S(2)}, u32[]{:S(2)}) collective-permute-start(f32[128,128]{1,0:T(8,128)S(1)} %slice.55), channel_id=1, source_target_pairs={{0,2},{2,4},{4,6},{6,8},{8,10},{10,12},{12,14},{14,0},{1,3},{3,5},... | collective-permute-start | bytes 196616 | tf_op jit(solution)/shard_map/ppermute | solution.py:60
  175.2 11.4 %collective-permute-start.19 = (f32[128,128]{1,0:T(8,128)S(1)}, f32[128,128]{1,0:T(8,128)S(1)}, u32[]{:S(2)}, u32[]{:S(2)}) collective-permute-start(f32[128,128]{1,0:T(8,128)S(1)} %slice.56), channel_id=1, source_target_pairs={{0,14},{2,0},{4,2},{6,4},{8,6},{10,8},{12,10},{14,12},{1,15},{3,1}... | collective-permute-start | bytes 196616 | tf_op jit(solution)/shard_map/ppermute | solution.py:61
  187.6 19.6 %all-to-all-start.5 = ((f32[4,2,224,128]{3,2,1,0:T(8,128)}), f32[4,2,224,128]{3,2,1,0:T(8,128)}, u32[]{:S(2)}, u32[]{:S(2)}) async-start(f32[4,2,224,128]{3,2,1,0:T(8,128)} %broadcast_in_dim.13), calls=%async_computation.5 | async-start | bytes 1835008 | tf_op jit(solution)/shard_map/all_to_all | solution.py:70
  207.2 12.1 %all-to-all-start.6 = ((f32[4,2,64,128]{3,2,1,0:T(8,128)}), f32[4,2,64,128]{3,2,1,0:T(8,128)}, u32[]{:S(2)}, u32[]{:S(2)}) async-start(f32[4,2,64,128]{3,2,1,0:T(8,128)} %copy.26), calls=%async_computation.6 | async-start | bytes 524288 | tf_op jit(solution)/shard_map/all_to_all | solution.py:380
  219.3 22.1 %all-to-all-start.7 = ((f32[16,2,2,32,128]{4,3,2,1,0:T(8,128)}), f32[16,2,2,32,128]{4,3,2,1,0:T(8,128)S(1)}, u32[]{:S(2)}, u32[]{:S(2)}) async-start(f32[16,2,2,32,128]{4,3,2,1,0:T(8,128)} %bitcast.107), calls=%async_computation.7 | async-start | bytes 2097152 | tf_op jit(solution)/shard_map/all_to_all | solution.py:422
  241.5 9.8 %collective-permute-start.24 = (f32[2,32,128]{2,1,0:T(8,128)S(1)}, f32[2,32,128]{2,1,0:T(8,128)S(1)}, u32[]{:S(2)}, u32[]{:S(2)}) collective-permute-start(f32[2,32,128]{2,1,0:T(8,128)S(1)} %get-tuple-element.83), channel_id=1, source_target_pairs={{0,0},{1,1},{2,16},{3,17},{4,32},{5,33},{6,48},{7,49},{8,8},{9,9},... | collective-permute-start | bytes 98312 | tf_op jit(solution)/shard_map/ppermute | solution.py:427
  257.5 11.5 %all-to-all-start.8 = ((f32[4,8,32,128]{3,2,1,0:T(8,128)}), f32[4,8,32,128]{3,2,1,0:T(8,128)S(1)}, u32[]{:S(2)}, u32[]{:S(2)}) async-start(f32[4,8,32,128]{3,2,1,0:T(8,128)} %broadcast_in_dim.14), calls=%async_computation.8 | async-start | bytes 1048576 | tf_op jit(solution)/shard_map/all_to_all | solution.py:70
  (36 other events, 412.3 us)
Sparse Core Ops, SparseCore 0:
  9.8 60.4 all-gather.5
  72.1 37.5 all-gather.7
  111.9 92.1 all-gather.9
